TPU v7x, 32 devices: a whole 2x2x4 slice. The times are simulated.
32 devices in a mesh: rep: 4 (over y, x), wide: 8 (over z, core).
Axes of the slice: x: 2, y: 2, z: 4, core: 2. Of those that a mesh axis runs over, the one named last changes fastest.
Arguments:
- token_ids: int32 [4, 1, 2, 1, 2048], P('rep'), may hold values from 0 to 50303, as said below
- prompt_mask: int32 [4, 1, 2, 1, 2048], P('rep'), may hold values from 0 to 1, as said below
- loss_pos: int32 [4, 1, 2, 8, 16], P('rep'), may hold values from 0 to 254
- tables: float32 [2, 50304, 512], P(None, 'wide', 'rep'), may hold values from -12 to 12
- attention: float32 [2, 2, 512, 512], P(None, None, 'wide', 'rep')
- feedforward: float32 [2, 2, 512, 2048], P(None, None, 'wide', 'rep')
- key_value: float32 [512, 128], P('wide', 'rep'), may hold values from -0.25 to 0.25
- gains_biases: float32 [12416], P('rep')
- first_tables: float32 [4, 2, 50304, 512], P('rep', None, 'wide'), may hold values from -5.8365434e-06 to 5.8365434e-06
- first_attention: float32 [4, 2, 2, 512, 512], P('rep', None, None, 'wide'), may hold values from -2.2888184e-05 to 2.2888184e-05
- first_feedforward: float32 [4, 2, 2, 512, 2048], P('rep', None, None, 'wide'), may hold values from -2.2888184e-05 to 2.2888184e-05
- first_key_value: float32 [4, 512, 128], P('rep', 'wide'), may hold values from -2.2888184e-05 to 2.2888184e-05
- first_gains: float32 [4, 12416], P('rep'), may hold values from -9.1552734e-05 to 9.1552734e-05
- second_tables: float32 [4, 2, 50304, 512], P('rep', None, 'wide'), may hold values from 9.2553283e-14 to 3.69509303e-11
- second_attention: float32 [4, 2, 2, 512, 512], P('rep', None, None, 'wide'), may hold values from 9.255328e-12 to 3.6950932e-11
- second_feedforward: float32 [4, 2, 2, 512, 2048], P('rep', None, None, 'wide'), may hold values from 9.255328e-12 to 3.6950932e-11
- second_key_value: float32 [4, 512, 128], P('rep', 'wide'), may hold values from 9.255328e-12 to 3.6950932e-11
- second_gains: float32 [4, 12416], P('rep'), may hold values from 1.759568e-10 to 7.038272e-10
- outer_tables: float32 [2, 50304, 512], P(None, 'wide', 'rep'), may hold values from -0.3125 to 0.3125
- outer_attention: float32 [2, 2, 512, 512], P(None, None, 'wide', 'rep'), may hold values from -0.3125 to 0.3125
- outer_feedforward: float32 [2, 2, 512, 2048], P(None, None, 'wide', 'rep'), may hold values from -0.3125 to 0.3125
- outer_key_value: float32 [512, 128], P('wide', 'rep'), may hold values from -0.3125 to 0.3125
- outer_gains: float32 [12416], P('rep'), may hold values from -0.3125 to 0.3125
Outputs:
- loss_sum: float32 [4], P('rep')
- loss_count: float32 [4], P('rep')
- new_tables: float32 [2, 50304, 512], P(None, 'wide', 'rep')
- new_attention: float32 [2, 2, 512, 512], P(None, None, 'wide', 'rep')
- new_feedforward: float32 [2, 2, 512, 2048], P(None, None, 'wide', 'rep')
- new_key_value: float32 [512, 128], P('wide', 'rep')
- new_gains: float32 [12416], P('rep')
- next_first_tables: float32 [4, 2, 50304, 512], P('rep', None, 'wide')
- next_first_attention: float32 [4, 2, 2, 512, 512], P('rep', None, None, 'wide')
- next_first_feedforward: float32 [4, 2, 2, 512, 2048], P('rep', None, None, 'wide')
- next_first_key_value: float32 [4, 512, 128], P('rep', 'wide')
- next_first_gains: float32 [4, 12416], P('rep')
- next_second_tables: float32 [4, 2, 50304, 512], P('rep', None, 'wide')
- next_second_attention: float32 [4, 2, 2, 512, 512], P('rep', None, None, 'wide')
- next_second_feedforward: float32 [4, 2, 2, 512, 2048], P('rep', None, None, 'wide')
- next_second_key_value: float32 [4, 512, 128], P('rep', 'wide')
- next_second_gains: float32 [4, 12416], P('rep')
- next_outer_tables: float32 [2, 50304, 512], P(None, 'wide', 'rep')
- next_outer_attention: float32 [2, 2, 512, 512], P(None, None, 'wide', 'rep')
- next_outer_feedforward: float32 [2, 2, 512, 2048], P(None, None, 'wide', 'rep')
- next_outer_key_value: float32 [512, 128], P('wide', 'rep')
- next_outer_gains: float32 [12416], P('rep')
Inputs may be any that keep to these rules, and one draw needn't show every extreme that they name: In each sequence prompt_mask is 0 before a prompt length under 2 * 2048 / 3 and 1 from there on. `token_ids`: vocabulary shard q holds the ids q * 6288 to (q + 1) * 6288 - 1. The 256 tokens of one device of wide in a micro-batch (places w * 256 to (w + 1) * 256 - 1 of every sequence) hold at most 64 ids of one shard, and in every micro-batch of a group some shard holds exactly 64 ids of every device's tokens.
All inputs are finite; a program needn't handle non-finite values.
Results may differ from a plain program's by a relative error of at most 0.012.
The roundings to bfloat16 on the way count: a program that leaves them out, or rounds other values in their place, can miss the bound.
Values may be sent and summed in bfloat16 or wider, within the bound.
No kernel may reach another device: no remote copies, remote signals or barrier semaphores. Data moves between devices by JAX's collectives and lax.ppermute only.
A program may use at most 448 MiB of HBM per device.

v0:
```python
from functools import partial

import jax
import jax.numpy as jnp
from jax import lax
from jax.experimental import pallas as pl
from jax.experimental.pallas import tpu as pltpu
from jax.sharding import Mesh
from jax.sharding import PartitionSpec as P

D = 512
HEADS = 8
HD = 64
ROT = 16
FF = 2048
L = 2
LEN = 2048
MICRO = 2
STEP = 5
WIDE_AXES = ("chip", "core")

NORM_EPSILON = 1e-05
CLIP = 0.1
LEARN_RATES = (0.02, 0.2, 0.02, 0.02, 0.2)
BETA_ONE = 0.9
BETA_TWO = 0.95
ADAM_EPSILON = 1e-08
DECAY = 0.1
OUTER_RATE = 0.7
OUTER_MOMENTUM = 0.9
FIX_ONE = 1.0 / (1.0 - BETA_ONE**STEP)
FIX_TWO = 1.0 / (1.0 - BETA_TWO**STEP)

BF = jnp.bfloat16
F4 = jnp.float32


def dot(left, right, dims):
    return lax.dot_general(left, right, (dims, ((), ())), preferred_element_type=F4)


def normal_of(stream):
    centred = stream - jnp.mean(stream, axis=-1, keepdims=True)
    scale = lax.rsqrt(jnp.mean(centred * centred, axis=-1, keepdims=True) + NORM_EPSILON)
    return centred * scale, scale


def norm_pull(shaped, normal, scale):
    return scale * (
        shaped
        - jnp.mean(shaped, axis=-1, keepdims=True)
        - normal * jnp.mean(shaped * normal, axis=-1, keepdims=True)
    )


def rotary(places):
    frequency = 10000.0 ** (-2.0 * jnp.arange(ROT // 2, dtype=F4) / ROT)
    angles = places.astype(F4)[:, None] * frequency[None, :]
    return jnp.cos(angles), jnp.sin(angles)


def rotate(values, cosine, sine):
    half = ROT // 2
    a = values[..., :half]
    b = values[..., half:ROT]
    c = cosine[:, None, :]
    s = sine[:, None, :]
    return jnp.concatenate([a * c - b * s, b * c + a * s, values[..., ROT:]], axis=-1)


def unpack_small(gains_biases):
    span = 7 * D + FF
    layers = gains_biases[: L * span].reshape(L, span)
    remain = gains_biases[L * span :]
    return layers, remain[: 2 * HD], remain[2 * HD : 2 * HD + D], remain[2 * HD + D :]


def moments_step(gradient, one, two):
    one = BETA_ONE * one + (1.0 - BETA_ONE) * gradient
    two = BETA_TWO * two + (1.0 - BETA_TWO) * gradient * gradient
    return one, two, (one * FIX_ONE) / (jnp.sqrt(two * FIX_TWO) + ADAM_EPSILON)


def step_of(one, two):
    two = two * FIX_TWO
    under = two * lax.rsqrt(jnp.maximum(two, 1e-37)) + ADAM_EPSILON
    guess = pl.reciprocal(under, approx=True)
    return one * FIX_ONE * (guess * (2.0 - under * guess))


def moments_fast(gradient, one, two):
    one = BETA_ONE * one + (1.0 - BETA_ONE) * gradient
    two = BETA_TWO * two + (1.0 - BETA_TWO) * gradient * gradient
    return one, two, step_of(one, two)


VM = pl.BlockSpec(memory_space=pltpu.VMEM)
SM = pl.BlockSpec(memory_space=pltpu.SMEM)
LANES = 128
BLOCKS = D // LANES
ROWS = 64
RUN = 2096
SPREAD = 4
FAR = 1 << 24


def shaped(*dims, kind=F4):
    return jax.ShapeDtypeStruct(dims, kind)


def takes(micros):
    return pl.CostEstimate(flops=0, bytes_accessed=int(micros * 3e6), transcendentals=0)


def call(kernel, outs, ins, smem=0, scratch=(), out_specs=None, name=None, room=63, far=(), cost=5):
    return pl.pallas_call(
        kernel,
        out_shape=outs,
        in_specs=[SM if i < smem else ANY if i in far else VM for i in range(len(ins))],
        out_specs=[VM] * len(outs) if out_specs is None else out_specs,
        scratch_shapes=list(scratch),
        compiler_params=pltpu.CompilerParams(vmem_limit_bytes=room * 1024 * 1024),
        name=name,
        cost_estimate=takes(cost),
    )(*ins)


ANY = pl.BlockSpec(memory_space=pltpu.HBM)
ATT = L * 2 * LANES
WIDE = 2 * FF // BLOCKS


class Fetch:
    def __init__(self, sc_ref, weights, scr, sems, start):
        w, rep = sc_ref[0], sc_ref[2]
        cols = pl.ds(start, scr.shape[2])
        self.copies = []
        for core in range(2):
            mine = weights[5 * core : 5 * core + 5]
            spots = [(mine[k], k, i, i) for k in range(3) for i in range(mine[0].shape[0])]
            cut = mine[3].shape[0]
            spots += [(mine[3], 3, i, i) for i in range(cut)]
            spots += [(mine[4], 3, i, i + cut) for i in range(mine[4].shape[0])]
            for ref, k, i, chip in spots:
                own_rows = ref.shape[1]
                at = pl.multiple_of((w ^ (2 * chip + core)) * own_rows, own_rows)
                self.copies.append(
                    pltpu.make_async_copy(
                        ref.at[i, :, cols],
                        scr.at[rep ^ k, pl.ds(at, own_rows), :],
                        sems.at[core, k, chip],
                    )
                )
        for copy in self.copies:
            copy.start()

    def wait(self):
        for copy in self.copies:
            copy.wait()


def nn(left, right):
    return dot(left, right, ((1,), (0,)))


def nt(left, right):
    return dot(left, right, ((1,), (1,)))


def tn(left, right):
    return dot(left, right, ((0,), (0,)))


def split_two(value):
    high = value.astype(BF)
    return high, (value - high.astype(F4)).astype(BF)


def lanes_of(rows):
    return lax.broadcasted_iota(jnp.int32, (rows, LANES), 1)


def spin(value, cosine, sine):
    place = lanes_of(value.shape[0]) % HD
    ahead = pltpu.roll(value, LANES - ROT // 2, 1)
    behind = pltpu.roll(value, ROT // 2, 1)
    moved = jnp.where(place < ROT // 2, -ahead, behind)
    return value * cosine + moved * sine


def swap_halves(value):
    return pltpu.roll(value, HD, 1)


def blocks_of(value):
    return [value[:, LANES * i : LANES * (i + 1)] for i in range(value.shape[1] // LANES)]


def tile_of(vr):
    return 2096 if vr % 2096 == 0 else vr


def stack_kernel(*refs):
    for i, ref in enumerate(refs[:-1]):
        refs[-1][i] = ref[...]


def lower_ones(size):
    first = lax.broadcasted_iota(jnp.int32, (size, size), 0)
    second = lax.broadcasted_iota(jnp.int32, (size, size), 1)
    return jnp.where(first <= second, 1.0, 0.0).astype(BF)


def rows_of(values, block):
    rows = [jnp.broadcast_to(value, (1, block)) for value in values]
    rows.append(jnp.zeros((8 - len(rows), block), F4))
    return jnp.concatenate(rows, axis=0).astype(BF)


def code_of(place, mb, width, seqs, rows_seq):
    m, b = lax.div(mb, width), lax.rem(mb, width)
    code = m * (seqs * LEN) + b * rows_seq
    return code + lax.div(place, rows_seq) * LEN + lax.rem(place, rows_seq)


def slots_kernel(
    seqs, rows_seq, vr, cap, sc_ref, own_all, x_all, y_all, d_all, ids_ref, code_ref, own_ref, rest_ref,
    all_ref,
):
    for k, ref in enumerate((own_all, x_all, y_all, d_all)):
        all_ref[k] = ref[...]
    groups = all_ref.shape[0]
    micros_width = ids_ref.shape[1] * LANES // cap
    block = all_ref.shape[2]
    width = micros_width // MICRO
    offset = sc_ref[3].astype(F4)
    per = LANES // cap
    lower = lower_ones(block)
    slot = lax.broadcasted_iota(jnp.int32, (LANES, 1), 0)
    wanted = (slot % cap).astype(F4)
    lane = lax.broadcasted_iota(jnp.int32, (1, LANES), 1)
    place = lax.broadcasted_iota(jnp.int32, (1, block), 1).astype(F4)

    def one(g, carry):
        local = all_ref[g, :micros_width, :] - offset
        inside = (local >= 0.0) & (local < vr)
        rank = nn(jnp.where(inside, 1.0, 0.0).astype(BF), lower) - 1.0
        rank = jnp.where(inside, rank, -1.0)
        local = jnp.where(inside, local, 0.0)
        high = jnp.floor(local * (1.0 / 64.0))
        for row in range(ids_ref.shape[1]):
            total = jnp.zeros((8, LANES), F4)
            for i in range(per):
                mb = row * per + i
                one_row = slice(mb, mb + 1)
                hot = (rank[one_row] == wanted) & (slot // cap == i)
                values = rows_of(
                    (high[one_row], local[one_row] - 64.0 * high[one_row], place, jnp.ones((1, 1), F4)),
                    block,
                )
                total = total + nt(values, jnp.where(hot, 1.0, 0.0).astype(BF))
            ids = (total[0:1] * 64.0 + total[1:2]).astype(jnp.int32)
            valid = total[3:4] > 0.5
            ids_ref[g, row : row + 1, :] = ids

            @pl.when(g == 0)
            def _():
                code = code_of(
                    total[2:3].astype(jnp.int32), row * per + lane // cap, width, seqs, rows_seq
                )
                code_ref[row : row + 1, :] = jnp.where(valid, code, FAR)
                own_ref[row : row + 1, :] = jnp.where(valid, ids, vr)
        return carry

    lax.fori_loop(0, groups, one, 0)
    for g in range(groups):
        rest_ref[sc_ref[2] ^ g] = all_ref[g, micros_width:, :]


def places_kernel(
    seqs, rows_seq, vr, cap, sc_ref, token_ref, mask_ref, loss_ref, slot_ref, own_ref, row_ref, turn_ref,
    key_out, chip_out, slot_out, row_out, target_out, weight_out, slot_cos, slot_sin, row_cos, row_sin,
):
    many, block = token_ref.shape
    width = many // MICRO
    n_loss = row_ref.shape[1]
    lrows = n_loss // many
    lower = lower_ones(block)
    tokens = token_ref[...]
    shard = jnp.floor((tokens + 0.5) * (1.0 / vr)).astype(jnp.int32) ^ sc_ref[0]
    rank = jnp.zeros((many, block), F4)
    for k in range(width):
        inside = jnp.where(shard == k, 1.0, 0.0)
        rank = rank + inside * (nn(inside.astype(BF), lower) - 1.0)
    spot = shard.astype(F4) * cap + rank
    wanted = lax.broadcasted_iota(jnp.int32, (width * cap, 1), 0).astype(F4)
    place = lax.broadcasted_iota(jnp.int32, (1, block), 1).astype(F4)
    values = rows_of((place, jnp.ones((1, 1), F4)), block)
    for mb in range(many):
        hot = jnp.where(spot[mb : mb + 1] == wanted, 1.0, 0.0).astype(BF)
        total = nt(values, hot)
        code = code_of(total[0:1].astype(jnp.int32), mb, width, seqs, rows_seq)
        code = jnp.where(total[1:2] > 0.5, code, FAR)
        key_out[mb] = code
        chip_out[mb] = code[:, : 2 * cap]
    high = jnp.floor(tokens * (1.0 / 256.0))
    low = tokens - 256.0 * high
    at = lax.broadcasted_iota(jnp.int32, (block, 1), 0)
    lane = lax.broadcasted_iota(jnp.int32, (1, LANES), 1)
    per = LANES // lrows
    for row in range(n_loss // LANES):
        codes = loss_ref[row : row + 1, :]
        after = lax.div(codes, rows_seq - 1) * rows_seq + lax.rem(codes, rows_seq - 1) + 1
        total = jnp.zeros((8, LANES), F4)
        for i in range(per):
            mb = slice(row * per + i, row * per + i + 1)
            hot = (at == after) & (lane // lrows == i)
            total = total + nn(
                rows_of((high[mb], low[mb], mask_ref[mb, :]), block),
                jnp.where(hot, 1.0, 0.0).astype(BF),
            )
        part = slice(LANES * row, LANES * (row + 1))
        target_out[0:1, part] = (total[0:1] * 256.0 + total[1:2]).astype(jnp.int32)
        weight_out[0:1, part] = total[2:3]

    def column(row):
        return jnp.transpose(jnp.broadcast_to(row, (LANES, LANES)))[:, 0:1]

    n_slots = slot_out.shape[0]
    ones = jnp.ones((HD - ROT, LANES), F4)
    zeros = jnp.zeros((HD - ROT, LANES), F4)
    ends = (jnp.ones((HD, LANES), F4), jnp.zeros((HD, LANES), F4))
    for start in range(0, n_slots + n_loss, LANES):
        slots = start < n_slots
        into = start if slots else start - n_slots
        part = slice(into, into + LANES)
        cosine = turn_ref[0:8, start : start + LANES]
        sine = turn_ref[8:16, start : start + LANES]
        cosines = [cosine, cosine, ones]
        sines = [sine, sine, zeros]
        cosines, sines = (
            (cosines + [ends[0]], sines + [ends[1]]) if slots else (cosines * 2, sines * 2)
        )
        cos_out, sin_out = (slot_cos, slot_sin) if slots else (row_cos, row_sin)
        cos_out[part, :] = jnp.transpose(jnp.concatenate(cosines, axis=0))
        sin_out[part, :] = jnp.transpose(jnp.concatenate(sines, axis=0))
        if slots:
            i = start // LANES
            slot_out[part, 0:1] = column(slot_ref[i : i + 1, :].astype(F4)).astype(jnp.int32)
            slot_out[part, 1:2] = column(own_ref[i : i + 1, :].astype(F4)).astype(jnp.int32)
        else:
            code = row_ref[0:1, part]
            row_out[part, 0:1] = column(code.astype(F4)).astype(jnp.int32)
            row_out[part, 1:2] = column((lax.div(code, LEN) * LEN).astype(F4)).astype(jnp.int32)


def kv_kernel(
    sc_ref, r0, r1, r2, r3, cos_ref, sin_ref, vec_ref, pair_bias_ref, slot_code_ref, row_ref, *refs
):
    pairs_ref, picked_ref, kv_ref, rows_ref = refs[-4:]
    n_slots = rows_ref.shape[1]
    for k, piece in enumerate((r0, r1, r2, r3)):
        rows_ref[sc_ref[2] ^ k] = piece[...]
    for k, piece in enumerate(refs[:-4]):
        own = piece.shape[0]
        kv_ref[pl.ds(pl.multiple_of((sc_ref[0] ^ k) * own, own), own), :] = piece[...]
    step = 256
    for start in range(0, n_slots, step):
        part = pl.ds(start, step)
        rows = jnp.concatenate([rows_ref[r, part, :] for r in range(BLOCKS)], axis=1)
        normal, unused = normal_of(rows.astype(F4))
        normed = (normal * vec_ref[0:1, :D] + vec_ref[0:1, D : 2 * D]).astype(BF)
        projected = pair_bias_ref[...] + nn(normed, kv_ref[...])
        pairs_ref[part, :] = spin(projected, cos_ref[part, :], sin_ref[part, :]).astype(BF)
    rows = jnp.concatenate([rows_ref[r] for r in range(BLOCKS)], axis=1)
    pick = jnp.where(row_ref[:, 0:1] == slot_code_ref[...], 1.0, 0.0).astype(BF)
    for r in range(BLOCKS):
        picked_ref[r] = nn(pick, rows[:, LANES * r : LANES * (r + 1)]).astype(BF)


def token_codes(place, m, first_block, seqs, rows_seq):
    block = seqs * rows_seq
    inside = lax.rem(place, block)
    code = m * (seqs * LEN) + (first_block + lax.div(place, block)) * rows_seq
    return code + lax.div(inside, rows_seq) * LEN + lax.rem(inside, rows_seq)


def order_kernel(seqs, rows_seq, width, cap, sc_ref, after_ref, code_ref, *refs):
    pieces, out_ref, stream_ref = refs[:-2], refs[-2], refs[-1]
    n_loss = stream_ref.shape[1]
    n_slots = MICRO * width * cap
    for core in range(2):
        for i in range(2):
            part = slice(n_slots + n_loss * i, n_slots + n_loss * (i + 1))
            total = pieces[core][part, :].astype(F4)
            for piece in pieces[core + 2 :: 2]:
                total = total + piece[part, :].astype(F4)
            stream_ref[2 * (sc_ref[1] ^ core) + i] = total
    block = seqs * rows_seq

    def one(mb, carry):
        m, b = lax.div(mb, width), lax.rem(mb, width)
        part = pl.ds(pl.multiple_of(mb * cap, cap), cap)
        slots = jnp.concatenate([piece[part, :] for piece in pieces], axis=0)
        place = lax.broadcasted_iota(jnp.int32, (block, 1), 0)
        hot = token_codes(place, m, b, seqs, rows_seq) == code_ref[mb]
        out_ref[mb] = nn(jnp.where(hot, 1.0, 0.0).astype(BF), slots).astype(BF)
        return carry

    lax.fori_loop(0, MICRO * width, one, 0)


def stack_heads(block_of, part):
    low_lanes = lanes_of(ROWS) < HD
    pieces = []
    for b in range(2):
        block = block_of[b, part, :]
        pieces += [block, swap_halves(block)]
    return [jnp.where(low_lanes, piece, 0.0) for piece in pieces]


def masks_of(row_ref, part, m, kt, tile, seqs, rows_seq):
    place = lax.broadcasted_iota(jnp.int32, (1, tile), 1)
    code = token_codes(place, m, kt * SPREAD, seqs, rows_seq)
    allowed = code <= row_ref[part, 0:1]
    if seqs > 1:
        allowed = allowed & (code >= row_ref[part, 1:2])
    return allowed


def masked(scores, allowed):
    return jnp.concatenate(
        [
            jnp.where(allowed, scores[ROWS * h : ROWS * (h + 1), :], -1e30)
            for h in range(HEADS // 2)
        ],
        axis=0,
    )


def attend(q_scr, ctx_ref, log_ref, keys_ref, row_ref, scr, seqs, rows_seq):
    micros, tiles, tile, unused = keys_ref.shape
    low_lanes = lanes_of(ROWS) < HD
    high = ROWS * HEADS // 2

    def one(t, carry):
        m, c = lax.div(t, tiles), lax.rem(t, tiles)
        part = pl.ds(pl.multiple_of(t * ROWS, ROWS), ROWS)
        query = jnp.concatenate(stack_heads(q_scr, part), axis=0).astype(BF)

        def scores_at(kt, top):
            allowed = masks_of(row_ref, part, m, kt, tile, seqs, rows_seq)
            scores = masked(nt(query, keys_ref[m, kt]), allowed)
            scr[kt] = scores
            for piece in blocks_of(scores):
                top = jnp.maximum(top, piece)
            return top

        top = lax.fori_loop(0, c + 1, scores_at, jnp.full((high, LANES), -1e30, F4))
        top = jnp.max(top, axis=1, keepdims=True)

        def expo_at(kt, total):
            expo = jnp.exp(scr[kt] - top)
            scr[kt] = expo
            for piece in blocks_of(expo):
                total = total + piece
            return total

        total = lax.fori_loop(0, c + 1, expo_at, jnp.zeros((high, LANES), F4))
        total = jnp.sum(total, axis=1, keepdims=True)
        inverse = 1.0 / total

        def context_at(kt, so_far):
            return so_far + nn((scr[kt] * inverse).astype(BF), keys_ref[m, kt])

        context = lax.fori_loop(0, c + 1, context_at, jnp.zeros((high, LANES), F4))
        log_ref[t] = top + jnp.log(total)
        heads = [context[ROWS * h : ROWS * (h + 1), :] for h in range(HEADS // 2)]
        for b in range(2):
            ctx_ref[b, part, :] = jnp.where(
                low_lanes, swap_halves(heads[2 * b]), heads[2 * b + 1]
            )
        return carry

    lax.fori_loop(0, micros * tiles, one, 0)


def attend_pull(
    q_ref, ctx_ref, grad_scr, log_ref, keys_ref, row_ref, dq_ref, dkv_ref, seqs, rows_seq
):
    micros, tiles, tile, unused = keys_ref.shape
    low_lanes = lanes_of(ROWS) < HD
    high = ROWS * HEADS // 2

    def one(t, carry):
        m, c = lax.div(t, tiles), lax.rem(t, tiles)
        part = pl.ds(pl.multiple_of(t * ROWS, ROWS), ROWS)
        query = jnp.concatenate(stack_heads(q_ref, part), axis=0).astype(BF)
        grads = []
        inners = []
        for b in range(2):
            grad = grad_scr[b, part, :]
            product = grad * ctx_ref[b, part, :]
            for sub in range(2):
                moved = swap_halves(grad) if sub == 0 else grad
                grads.append(jnp.where(low_lanes, 0.0, moved))
                mine = low_lanes if sub == 0 else ~low_lanes
                inners.append(jnp.sum(jnp.where(mine, product, 0.0), axis=1, keepdims=True))
        grad = jnp.concatenate(grads, axis=0).astype(BF)
        inner = jnp.concatenate(inners, axis=0)
        log_total = log_ref[t]

        def pull_at(kt, so_far):
            both = keys_ref[m, kt]
            allowed = masks_of(row_ref, part, m, kt, tile, seqs, rows_seq)
            probs = jnp.exp(masked(nt(query, both), allowed) - log_total)
            grad_scores = (probs * (nt(grad, both) - inner)).astype(BF)
            dkv_ref[m, kt] += tn(grad_scores, query) + tn(probs.astype(BF), grad)
            return so_far + nn(grad_scores, both)

        total = lax.fori_loop(0, c + 1, pull_at, jnp.zeros((high, LANES), F4)) * 0.125
        heads = [total[ROWS * h : ROWS * (h + 1), :] for h in range(HEADS // 2)]
        for b in range(2):
            dq_ref[b, part, :] = jnp.where(
                low_lanes, heads[2 * b], swap_halves(heads[2 * b + 1])
            ).astype(BF)
        return carry

    lax.fori_loop(0, micros * tiles, one, 0)


def to_slots(dkv_ref, code_ref, own_out, near_out, seqs, rows_seq):
    micros, tiles, tile, unused = dkv_ref.shape
    block = seqs * rows_seq
    width = tiles * SPREAD
    cap = own_out.shape[0] // (micros * width)

    def one(mb, carry):
        m, b = lax.div(mb, width), lax.rem(mb, width)
        part = pl.ds(pl.multiple_of(mb * cap, cap), cap)
        inside = pl.ds(pl.multiple_of(lax.rem(b, SPREAD) * block, block), block)
        high, rest = split_two(dkv_ref[m, lax.div(b, SPREAD), inside, :])
        place = lax.broadcasted_iota(jnp.int32, (block, 1), 0)
        code = token_codes(place, m, b, seqs, rows_seq)
        hot = jnp.where(code == code_ref[mb], 1.0, 0.0).astype(BF)
        both = tn(hot, high) + tn(hot, rest)
        own_out[part, :] = both[:cap, :]
        near_out[part, :] = both[cap:, :]
        return carry

    lax.fori_loop(0, micros * width, one, 0)


def join_blocks(parity, own_ref, other_ref):
    return [
        jnp.where(parity == r // 2, own_ref[r % 2].astype(F4), other_ref[r % 2].astype(F4))
        for r in range(BLOCKS)
    ]


def branch_of(parity, k, own_ref, other_ref, att_ref):
    context = jnp.concatenate(join_blocks(parity, own_ref, other_ref), axis=1).astype(BF)
    at = k * 256 + LANES
    return jnp.concatenate(
        [nn(context, att_ref[r, :, at : at + LANES]) for r in range(BLOCKS)], axis=1
    )


def queries_of(k, stream, parity, vec_ref, att_ref, cos_ref, sin_ref, q_ref):
    normal, unused = normal_of(stream)
    normed = (normal * vec_ref[0:1, :D] + vec_ref[0:1, D : 2 * D]).astype(BF)
    cosine, sine = cos_ref[...], sin_ref[...]
    for i in range(2):
        weight = jnp.where(
            parity == 0,
            att_ref[i, :, k * 256 : k * 256 + LANES],
            att_ref[2 + i, :, k * 256 : k * 256 + LANES],
        )
        low = vec_ref[0:1, 4 * D + LANES * i : 4 * D + LANES * (i + 1)]
        high = vec_ref[0:1, 4 * D + LANES * (2 + i) : 4 * D + LANES * (3 + i)]
        query = nn(normed, weight) + jnp.where(parity == 0, low, high)
        query = spin(query, cosine, sine).astype(BF).astype(F4)
        q_ref[i] = query * 0.125


def first_kernel(
    seqs, rows_seq, sc_ref, low_ref, vec_ref, w0, w1, w2, w3, w4, w5, w6, w7, w8, w9, keys_ref, row_ref, cos_ref, sin_ref,
    stream_ref, q_ref, ctx_ref, log_ref, scr, att_ref, sem,
):
    copy = Fetch(sc_ref, (w0, w1, w2, w3, w4, w5, w6, w7, w8, w9), att_ref, sem, L * WIDE)
    stream_ref[...] = jnp.concatenate([low_ref[r] for r in range(BLOCKS)], axis=1)
    copy.wait()
    queries_of(0, stream_ref[...], sc_ref[1], vec_ref, att_ref, cos_ref, sin_ref, q_ref)
    attend(q_ref, ctx_ref, log_ref, keys_ref, row_ref, scr, seqs, rows_seq)


def second_kernel(
    seqs, rows_seq, sc_ref, partial_ref, own_ref, other_ref, vec_ref, w0, w1, w2, w3, w4, w5, w6, w7, w8, w9, keys_ref, row_ref,
    cos_ref, sin_ref, stream_ref, q_ref, ctx_ref, log_ref, scr, att_ref, sem,
):
    parity = sc_ref[1]
    Fetch(sc_ref, (w0, w1, w2, w3, w4, w5, w6, w7, w8, w9), att_ref, sem, L * WIDE).wait()
    stream_ref[...] = partial_ref[...] + branch_of(parity, 0, own_ref, other_ref, att_ref)
    queries_of(1, stream_ref[...], parity, vec_ref, att_ref, cos_ref, sin_ref, q_ref)
    attend(q_ref, ctx_ref, log_ref, keys_ref, row_ref, scr, seqs, rows_seq)


ROOT_HALF = 0.7071067811865476
ROOT_TAU = 0.3989422804014327


def feed_kernel(k, sc_ref, stream_ref, vec_ref, w0, w1, w2, w3, w4, w5, w6, w7, w8, w9, out_ref, ff_ref, sem):
    copy = Fetch(sc_ref, (w0, w1, w2, w3, w4, w5, w6, w7, w8, w9), ff_ref, sem, k * WIDE)
    stream = stream_ref[...]
    normal, unused = normal_of(stream)
    feed = (normal * vec_ref[0:1, 2 * D : 3 * D] + vec_ref[0:1, 3 * D : 4 * D]).astype(BF)
    total = stream + vec_ref[0:1, 5 * D : 6 * D] + vec_ref[0:1, 6 * D : 7 * D]
    cols = FF // BLOCKS
    copy.wait()
    for r in range(BLOCKS):
        at_r = 7 * D + cols * r
        hidden = nn(feed, ff_ref[r, :, :cols]) + vec_ref[0:1, at_r : at_r + cols]
        active = (0.5 * hidden * (1.0 + lax.erf(hidden * ROOT_HALF))).astype(BF)
        total = total + nt(active, ff_ref[r, :, cols:])
    out_ref[...] = total


def runs_of(tables_ref):
    vr = tables_ref.shape[1]
    step = RUN if vr % RUN == 0 else vr
    for start in range(0, vr, step):
        part = slice(start, start + step)
        yield start, step, jnp.concatenate([tables_ref[r, part, :] for r in range(BLOCKS)], axis=1)


def logits_kernel(
    sc_ref, partial_ref, own_ref, other_ref, w0, w1, w2, w3, w4, w5, w6, w7, w8, w9, final_ref, target_ref, tables_ref,
    logits_ref, stats_ref, stream_ref, picked_ref, att_ref, sem,
):
    parity, offset = sc_ref[1], sc_ref[3]
    Fetch(sc_ref, (w0, w1, w2, w3, w4, w5, w6, w7, w8, w9), att_ref, sem, L * WIDE).wait()
    stream = partial_ref[...] + branch_of(parity, 1, own_ref, other_ref, att_ref)
    stream_ref[...] = stream
    normal, unused = normal_of(stream)
    picked = (normal * final_ref[0:1, :] + final_ref[1:2, :]).astype(BF)
    picked_ref[...] = picked
    n_loss = picked.shape[0]
    top = jnp.full((1, n_loss), -1e30, F4)
    hit_total = jnp.zeros((1, n_loss), F4)
    target = target_ref[...] - offset
    for start, size, table in runs_of(tables_ref):
        logits = nt(table, picked)
        logits_ref[start : start + size, :] = logits
        top = jnp.maximum(top, jnp.max(logits, axis=0, keepdims=True))
        place = lax.broadcasted_iota(jnp.int32, (size, n_loss), 0) + start
        hit_total = hit_total + jnp.sum(
            jnp.where(place == target, logits, 0.0), axis=0, keepdims=True
        )
    total = jnp.zeros((1, n_loss), F4)
    step = tile_of(logits_ref.shape[0])
    for start in range(0, logits_ref.shape[0], step):
        total = total + jnp.sum(
            jnp.exp(logits_ref[start : start + step, :] - top), axis=0, keepdims=True
        )
    stats_ref[0:1, :] = top
    stats_ref[1:2, :] = total
    stats_ref[2:3, :] = hit_total
    stats_ref[3:8, :] = jnp.zeros((5, n_loss), F4)


def join_stats(one, two):
    top = jnp.maximum(one[0], two[0])
    total = one[1] * jnp.exp(one[0] - top) + two[1] * jnp.exp(two[0] - top)
    return top, total, one[2] + two[2]


def probs_kernel(
    sc_ref, stats_ref, weight_ref, target_ref, logits_ref, tables_ref, probs_ref, grad_ref,
    loss_ref,
):
    offset = sc_ref[3]
    vr, n_loss = logits_ref.shape
    parts = [tuple(stats_ref[k, i : i + 1, :] for i in range(3)) for k in range(stats_ref.shape[0])]
    while len(parts) > 1:
        parts = [join_stats(parts[i], parts[i + 1]) for i in range(0, len(parts), 2)]
    top, total, hit = parts[0]
    log_all = top + jnp.log(total)
    weight = weight_ref[...]
    loss_ref[0, 0] = jnp.sum(weight * (log_all - hit))
    share = weight / jnp.sum(weight)
    target = target_ref[...] - offset
    grads = jnp.zeros((n_loss, D), F4)
    for start, size, table in runs_of(tables_ref):
        place = lax.broadcasted_iota(jnp.int32, (size, n_loss), 0) + start
        probs = jnp.exp(logits_ref[start : start + size, :] - log_all)
        probs = (jnp.where(place == target, probs - 1.0, probs) * share).astype(BF)
        probs_ref[start : start + size, :] = probs
        grads = grads + tn(probs, table)
    for r in range(BLOCKS):
        grad_ref[r] = grads[:, LANES * r : LANES * (r + 1)]


def squares_kernel(probs_ref, picked_ref, out_ref):
    vr = probs_ref.shape[0]
    tile = tile_of(vr)
    total = jnp.zeros((), F4)
    for start in range(0, vr, tile):
        grads = nn(probs_ref[start : start + tile, :], picked_ref[...])
        total = total + jnp.sum(grads * grads)
    out_ref[0, 0] = total


def layer_pull(
    k, seqs, rows_seq, sc_ref, grad_stream, stream, vec_ref, att_ref, ff_ref, copy, own_ref, other_ref, q_ref,
    log_ref, keys_ref, row_ref, dq_ref, dkv_ref, wide_ref, out_ref, vec_out,
    feed_scr, low_scr, grad_scr, prod_scr, square,
):
    parity = sc_ref[1]
    block, place = sc_ref[4], sc_ref[5]
    rows = wide_ref.shape[1]
    cols = FF // BLOCKS
    normal, unused = normal_of(stream)
    feed = (normal * vec_ref[0:1, 2 * D : 3 * D] + vec_ref[0:1, 3 * D : 4 * D]).astype(BF)
    low = grad_stream.astype(BF)
    for r in range(BLOCKS):
        feed_scr[r] = feed[:, LANES * r : LANES * (r + 1)]
        low_scr[r] = low[:, LANES * r : LANES * (r + 1)]
    feed_own = feed_scr[block]
    low_own = low_scr[block]

    at = k * 256 + LANES
    half = D // 2
    start = pl.ds(pl.multiple_of(parity * half, half), half)
    grad_context = nt(low_scr[0], att_ref[0, start, at : at + LANES])
    for r in range(1, BLOCKS):
        grad_context = grad_context + nt(low_scr[r], att_ref[r, start, at : at + LANES])
    grad_context = grad_context.astype(BF).astype(F4)
    grad_scr[0] = grad_context[:, :LANES]
    grad_scr[1] = grad_context[:, LANES:]
    attend_pull(
        q_ref, own_ref, grad_scr, log_ref, keys_ref, row_ref, dq_ref, dkv_ref, seqs,
        rows_seq,
    )

    vec_out[0:1, 5 * D : 6 * D] = jnp.sum(low.astype(F4), axis=0, keepdims=True)
    vec_out[0:1, 6 * D : 7 * D] = jnp.sum(low.astype(F4), axis=0, keepdims=True)
    grad_feed = jnp.zeros_like(grad_stream)
    copy.wait()
    for r in range(BLOCKS):
        at_r = 7 * D + cols * r
        hidden = nn(feed, ff_ref[r, :, :cols]) + vec_ref[0:1, at_r : at_r + cols]
        grown = 1.0 + lax.erf(hidden * ROOT_HALF)
        active = (0.5 * hidden * grown).astype(BF)
        slope = 0.5 * grown + hidden * (ROOT_TAU * jnp.exp(-0.5 * hidden * hidden))
        grad_hidden = (nn(low, ff_ref[r, :, cols:]) * slope).astype(BF)
        grad_feed = grad_feed + nt(grad_hidden, ff_ref[r, :, :cols])
        vec_out[0:1, at_r : at_r + cols] = jnp.sum(
            grad_hidden.astype(F4), axis=0, keepdims=True
        )
        for which, product in enumerate((tn(feed_own, grad_hidden), tn(low_own, active))):
            prod_scr[...] = product
            piece = prod_scr[pl.ds(pl.multiple_of(place, 16), rows), :]
            wide_ref[which, :, cols * r : cols * (r + 1)] = piece
            square = square + jnp.sum(piece * piece)
    blocks = join_blocks(parity, own_ref, other_ref)
    context_own = blocks[0]
    for r in range(1, BLOCKS):
        context_own = jnp.where(block == r, blocks[r], context_own)
    prod_scr[...] = tn(context_own.astype(BF), low)
    piece = prod_scr[pl.ds(pl.multiple_of(place, 16), rows), :]
    out_ref[...] = piece
    square = square + jnp.sum(piece * piece)
    vec_out[0:1, 2 * D : 3 * D] = jnp.sum(grad_feed * normal, axis=0, keepdims=True)
    vec_out[0:1, 3 * D : 4 * D] = jnp.sum(grad_feed, axis=0, keepdims=True)
    return grad_feed, square


def query_pull(
    k, sc_ref, stream, grad_feed, own_ref, other_ref, vec_ref, att_ref, cos_ref, sin_ref, wq_ref,
    head_out, normed_scr, prod_scr, square,
):
    parity = sc_ref[1]
    block, place = sc_ref[4], sc_ref[5]
    rows = wq_ref.shape[0]
    normal, scale = normal_of(stream)
    normed = (normal * vec_ref[0:1, :D] + vec_ref[0:1, D : 2 * D]).astype(BF)
    for r in range(BLOCKS):
        normed_scr[r] = normed[:, LANES * r : LANES * (r + 1)]
    cosine, sine = cos_ref[...], sin_ref[...]
    grad_normed = jnp.zeros_like(stream)
    pieces = []
    for r, part in enumerate(join_blocks(parity, own_ref, other_ref)):
        piece = spin(part.astype(F4), cosine, -sine).astype(BF)
        head_out[0:1, 2 * D + LANES * r : 2 * D + LANES * (r + 1)] = jnp.sum(
            piece.astype(F4), axis=0, keepdims=True
        )
        grad_normed = grad_normed + nt(piece, att_ref[r, :, k * 256 : k * 256 + LANES])
        pieces.append(piece)
    prod_scr[...] = tn(normed_scr[block], jnp.concatenate(pieces, axis=1))
    piece = prod_scr[pl.ds(pl.multiple_of(place, 16), rows), :]
    wq_ref[...] = piece
    square = square + jnp.sum(piece * piece)
    head_out[0:1, :D] = jnp.sum(grad_normed * normal, axis=0, keepdims=True)
    head_out[0:1, D : 2 * D] = jnp.sum(grad_normed, axis=0, keepdims=True)
    shaped_all = grad_normed * vec_ref[0:1, :D] + grad_feed * vec_ref[0:1, 2 * D : 3 * D]
    return norm_pull(shaped_all, normal, scale), square


def last_pull_kernel(
    seqs, rows_seq, sc_ref, before_ref, grads_ref, final_ref, final_stream_ref, stream_ref, vec_ref, w0, w1, w2, w3, w4, w5, w6, w7, w8, w9,
    own_ref, other_ref, q_ref, log_ref, keys_ref, row_ref, dq_ref, dkv_ref,
    wide_ref, out_ref, vec_out, final_out, grad_out, feed_out, square_ref, feed_scr, low_scr,
    grad_scr, prod_scr, att_ref, ff_ref, sems,
):
    att_copy = Fetch(sc_ref, (w0, w1, w2, w3, w4, w5, w6, w7, w8, w9), att_ref, sems.at[0], L * WIDE)
    copy = Fetch(sc_ref, (w0, w1, w2, w3, w4, w5, w6, w7, w8, w9), ff_ref, sems.at[1], WIDE)
    grad_picked = jnp.concatenate([grads_ref[r] for r in range(BLOCKS)], axis=1)
    normal, scale = normal_of(final_stream_ref[...])
    final_out[0:1, :] = jnp.sum(grad_picked * normal, axis=0, keepdims=True)
    final_out[1:2, :] = jnp.sum(grad_picked, axis=0, keepdims=True)
    grad_stream = norm_pull(grad_picked * final_ref[0:1, :], normal, scale)
    grad_out[...] = grad_stream
    dkv_ref[...] = jnp.zeros_like(dkv_ref)
    att_copy.wait()
    grad_feed, square = layer_pull(
        1, seqs, rows_seq, sc_ref, grad_stream, stream_ref[...], vec_ref, att_ref, ff_ref, copy, own_ref,
        other_ref, q_ref, log_ref, keys_ref, row_ref, dq_ref, dkv_ref,
        wide_ref, out_ref, vec_out, feed_scr, low_scr, grad_scr, prod_scr, before_ref[0, 0],
    )
    feed_out[...] = grad_feed
    square_ref[0, 0] = square


def first_pull_kernel(
    seqs, rows_seq, sc_ref, grad_in_ref, feed_in_ref, dq_own_ref, dq_other_ref, stream1_ref, vec1_ref,
    stream_ref, vec_ref, w0, w1, w2, w3, w4, w5, w6, w7, w8, w9, own_ref, other_ref, q_ref, log_ref, keys_ref,
    row_ref, cos_ref, sin_ref, dkv_in_ref, chip_code_ref, dq_ref, own_slots,
    near_slots, wide_ref, out_ref, vec_out, wq_ref, head_out, grad_out, feed_out, square_ref, feed_scr,
    low_scr, grad_scr, prod_scr, dkv_ref, att_ref, ff_ref, sems, dkv_sem,
):
    dkv_copy = pltpu.make_async_copy(dkv_in_ref, dkv_ref, dkv_sem)
    dkv_copy.start()
    att_copy = Fetch(sc_ref, (w0, w1, w2, w3, w4, w5, w6, w7, w8, w9), att_ref, sems.at[0], L * WIDE)
    copy = Fetch(sc_ref, (w0, w1, w2, w3, w4, w5, w6, w7, w8, w9), ff_ref, sems.at[1], 0)
    att_copy.wait()
    grad_part, square = query_pull(
        1, sc_ref, stream1_ref[...], feed_in_ref[...], dq_own_ref, dq_other_ref, vec1_ref, att_ref,
        cos_ref, sin_ref, wq_ref, head_out, feed_scr, prod_scr, jnp.zeros((), F4),
    )
    grad_stream = grad_in_ref[...] + grad_part
    grad_out[...] = grad_stream
    dkv_copy.wait()
    grad_feed, square = layer_pull(
        0, seqs, rows_seq, sc_ref, grad_stream, stream_ref[...], vec_ref, att_ref, ff_ref, copy, own_ref,
        other_ref, q_ref, log_ref, keys_ref, row_ref, dq_ref, dkv_ref,
        wide_ref, out_ref, vec_out, feed_scr, low_scr, grad_scr, prod_scr, square,
    )
    to_slots(dkv_ref, chip_code_ref, own_slots, near_slots, seqs, rows_seq)
    feed_out[...] = grad_feed
    square_ref[0, 0] = square


def embed_pull_kernel(
    sc_ref, grad_in_ref, feed_in_ref, dq_own_ref, dq_other_ref, stream_ref, vec_ref, w0, w1, w2, w3, w4, w5, w6, w7, w8, w9, kv_ref,
    cos_ref, sin_ref, dkv_own_ref, dkv_other_ref, rows_ref, slot_cos_ref, slot_sin_ref,
    slot_ref, row_code_ref, id_row_ref, wq_ref, head_out, rows_out, ids_out,
    kv_out, gain_out, square_ref, count_ref, normed_scr, prod_scr, high_scr, low_scr, att_ref, sem,
):
    Fetch(sc_ref, (w0, w1, w2, w3, w4, w5, w6, w7, w8, w9), att_ref, sem, L * WIDE).wait()
    grad_part, square = query_pull(
        0, sc_ref, stream_ref[...], feed_in_ref[...], dq_own_ref, dq_other_ref, vec_ref, att_ref,
        cos_ref, sin_ref, wq_ref, head_out, normed_scr, prod_scr, jnp.zeros((), F4),
    )
    grad_high, grad_low = split_two(grad_in_ref[...] + grad_part)
    n_slots = rows_ref.shape[1]
    step = 256
    kv_total = jnp.zeros((D, LANES), F4)
    gain_total = jnp.zeros((1, D), F4)
    bias_total = jnp.zeros((1, D), F4)
    pair_total = jnp.zeros((1, LANES), F4)
    gain = vec_ref[0:1, :D]
    for start in range(0, n_slots, step):
        part = pl.ds(start, step)
        real = slot_ref[part, 0:1] < FAR
        grad_pair = dkv_own_ref[part, :] + dkv_other_ref[part, :]
        grad_pair = grad_pair.astype(BF).astype(F4)
        grad_pair = spin(grad_pair, slot_cos_ref[part, :], -slot_sin_ref[part, :])
        grad_pair = jnp.where(real, grad_pair, 0.0).astype(BF)
        rows = jnp.concatenate([rows_ref[r, part, :] for r in range(BLOCKS)], axis=1)
        normal, scale = normal_of(rows.astype(F4))
        normed = (normal * gain + vec_ref[0:1, D : 2 * D]).astype(BF)
        kv_total = kv_total + tn(normed, grad_pair)
        pair_total = pair_total + jnp.sum(grad_pair.astype(F4), axis=0, keepdims=True)
        grad_normed = nt(grad_pair, kv_ref[...])
        gain_total = gain_total + jnp.sum(grad_normed * normal, axis=0, keepdims=True)
        bias_total = bias_total + jnp.sum(grad_normed, axis=0, keepdims=True)
        pick = (slot_ref[part, 0:1] == row_code_ref[...]).astype(F4).astype(BF)
        grad_rows = norm_pull(grad_normed * gain, normal, scale)
        grad_rows = grad_rows + (nn(pick, grad_high) + nn(pick, grad_low))
        grad_rows = jnp.where(real, grad_rows, 0.0)
        high_scr[part, :], low_scr[part, :] = split_two(grad_rows)
    kv_out[...] = kv_total
    gain_out[0:1, :] = gain_total
    gain_out[1:2, :] = bias_total
    gain_out[2:3, :] = jnp.concatenate([pair_total, jnp.zeros((1, D - LANES), F4)], axis=1)
    gain_out[3:8, :] = jnp.zeros((5, D), F4)
    vr = sc_ref[6]
    ids = id_row_ref[...]
    spot = lax.broadcasted_iota(jnp.int32, (1, n_slots), 1)
    later = jnp.zeros((1, n_slots), F4)
    for start in range(0, n_slots, step):
        at = lax.broadcasted_iota(jnp.int32, (step, 1), 0) + start
        same = (slot_ref[pl.ds(start, step), 1:2] == ids) & (at < spot)
        later = jnp.maximum(later, jnp.max(jnp.where(same, 1.0, 0.0), axis=0, keepdims=True))
    lead = jnp.where(ids < vr, 1.0 - later, 0.0)
    rank = jnp.zeros((8, n_slots), F4)
    many = jnp.broadcast_to(lead, (8, n_slots)).astype(BF)
    for start in range(0, n_slots, step):
        before = jnp.where(slot_ref[pl.ds(start, step), 1:2] < ids, 1.0, 0.0).astype(BF)
        rank = rank + nn(many[:, start : start + step], before)
    rank = jnp.where(lead > 0.0, rank[0:1, :].astype(jnp.int32), -1)
    count_ref[0, 0] = jnp.sum(lead).astype(jnp.int32)
    for start in range(0, n_slots, step):
        part = pl.ds(start, step)
        at = lax.broadcasted_iota(jnp.int32, (step, 1), 0) + start
        packed = jnp.max(jnp.where(rank == at, ids, -1), axis=1, keepdims=True)
        ids_out[part, :] = packed
        hot = jnp.where(packed == ids, 1.0, 0.0).astype(BF)
        total = nn(hot, high_scr[...]) + nn(hot, low_scr[...])
        rows_out[part, :] = total.astype(BF)
        square = square + jnp.sum(total * total)
    square_ref[0, 0] = square


TILE = 528
SETTLE = 1056


def params():
    return pltpu.CompilerParams(vmem_limit_bytes=63 * 1024 * 1024)


def base_kernel(first_ref, second_ref, after_ref, step_ref):
    one = BETA_ONE * first_ref[0, 0]
    two = BETA_TWO * second_ref[0, 0]
    step = step_of(one, two)
    for r in range(BLOCKS):
        step_ref[r] = step[:, LANES * r : LANES * (r + 1)].astype(BF)


def base_pass(first, second, after):
    vr = first.shape[2]
    whole = pl.BlockSpec((1, 1, SETTLE, D), lambda i: (0, 0, i, 0))
    return pl.pallas_call(
        base_kernel,
        grid=(pl.cdiv(vr, SETTLE),),
        in_specs=[whole, whole, pl.BlockSpec((16, LANES), lambda i: (0, 0))],
        out_specs=pl.BlockSpec((BLOCKS, SETTLE, LANES), lambda i: (0, i, 0)),
        out_shape=shaped(BLOCKS, vr, LANES, kind=BF),
        compiler_params=params(),
        name="embedding_base",
        cost_estimate=takes(14),
    )(first, second, after)


def unembed_kernel(clip_ref, probs_ref, picked_ref, first_ref, second_ref, *refs):
    one_ref, two_ref, step_ref = refs[-3:]
    gradient = nn(probs_ref[...], picked_ref[...]) * clip_ref[0]
    one, two, step = moments_fast(gradient, first_ref[0, 0], second_ref[0, 0])
    one_ref[0, 0] = one
    two_ref[0, 0] = two
    for r in range(BLOCKS):
        step_ref[r] = step[:, LANES * r : LANES * (r + 1)].astype(BF)


def unembed_pass(clip, probs, picked, first, second, held, start, count):
    vr, n_loss = probs.shape
    rows = min(vr, (start + count) * TILE) - start * TILE
    whole = pl.BlockSpec((1, 1, TILE, D), lambda i: (0, 1, i + start, 0))
    return pl.pallas_call(
        unembed_kernel,
        grid=(count,),
        in_specs=[
            SM,
            pl.BlockSpec((TILE, n_loss), lambda i: (i + start, 0)),
            pl.BlockSpec((n_loss, D), lambda i: (0, 0)),
            whole,
            whole,
        ]
        + [ANY] * len(held),
        out_specs=[whole, whole, pl.BlockSpec((BLOCKS, TILE, LANES), lambda i: (0, i, 0))],
        out_shape=[shaped(*first.shape)] * 2 + [shaped(BLOCKS, rows, LANES, kind=BF)],
        input_output_aliases={5 + i: i for i in range(len(held))},
        compiler_params=params(),
        name="unembedding_adam",
        cost_estimate=takes(16),
    )(clip, probs, picked, first, second, *held)


GROUP = 128


def overlapping(id_at, count, first, tile, step):
    def one(i, carry):
        least = id_at(i * GROUP)
        most = id_at(jnp.minimum(i * GROUP + GROUP, count) - 1)

        @pl.when((least < first + tile) & (most >= first))
        def _():
            step(i, pl.ds(pl.multiple_of(i * GROUP, GROUP), GROUP))

        return carry

    lax.fori_loop(0, lax.div(count + GROUP - 1, GROUP), one, 0)


def embed_kernel(
    start, last, clip_ref, count_ref, at_ref, id_ref, col_ref, rows_ref, first_ref, second_ref, base_ref,
    *refs,
):
    one_ref, two_ref, extra_ref, scr, extra_scr = refs[-5:]
    tile = one_ref.shape[2]
    first = (pl.program_id(0) + start) * tile
    place = lax.broadcasted_iota(jnp.int32, (tile, 1), 0) + first
    row = lax.broadcasted_iota(jnp.int32, (1, tile), 1) + first

    @pl.when(pl.program_id(0) == 0)
    def _():
        extra_ref[...] = jnp.zeros_like(extra_ref)

    scr[...] = jnp.zeros_like(scr)

    def gather(i, part):
        hot = jnp.where(place == id_ref[i], 1.0, 0.0).astype(BF)
        scr[...] += nn(hot, rows_ref[part, :])

    overlapping(lambda k: at_ref[k], count_ref[0], first, tile, gather)
    one, two, step = moments_fast(scr[...] * clip_ref[0], first_ref[0, 0], second_ref[0, 0])
    one_ref[0, 0] = one
    two_ref[0, 0] = two
    base = jnp.concatenate([base_ref[r] for r in range(BLOCKS)], axis=1).astype(F4)
    extra_scr[...] = jnp.where(place < last, step - base, 0.0).astype(BF)

    def scatter(i, part):
        hot = jnp.where(row == col_ref[part, :], 1.0, 0.0).astype(BF)
        picked = nn(hot, extra_scr[...])
        for r in range(BLOCKS):
            extra_ref[r, part, :] += picked[:, LANES * r : LANES * (r + 1)]

    overlapping(lambda k: at_ref[k], count_ref[0], first, tile, scatter)


def embed_pass(clip, count, ids, rows, first, second, base, held, after, start, tiles):
    n_slots = rows.shape[0]
    vr = first.shape[2]
    whole = pl.BlockSpec((1, 1, TILE, D), lambda i: (0, 0, i + start, 0))
    blocks = pl.BlockSpec((BLOCKS, n_slots, LANES), lambda i: (0, 0, 0))
    groups = n_slots // GROUP
    return pl.pallas_call(
        partial(embed_kernel, start, vr),
        grid=(tiles,),
        in_specs=[
            SM,
            SM,
            SM,
            pl.BlockSpec((groups, 1, GROUP), lambda i: (0, 0, 0)),
            pl.BlockSpec((n_slots, 1), lambda i: (0, 0)),
            pl.BlockSpec((n_slots, D), lambda i: (0, 0)),
            whole,
            whole,
            pl.BlockSpec((BLOCKS, TILE, LANES), lambda i: (0, i + start, 0)),
        ]
        + [ANY] * 3,
        out_specs=[whole, whole, blocks],
        out_shape=[shaped(*first.shape)] * 2 + [shaped(BLOCKS, n_slots, LANES)],
        input_output_aliases={9: 0, 10: 1},
        scratch_shapes=[pltpu.VMEM((TILE, D), F4), pltpu.VMEM((TILE, D), BF)],
        compiler_params=params(),
        name="embedding_adam",
        cost_estimate=takes(17),
    )(clip, count, ids.reshape(-1), ids.reshape(groups, 1, GROUP), ids, rows, first, second, base, *held, after)


def layers_kernel(
    clip_ref, after_ref, wq0, out0, wq1, out1, wide0, wide1, kv_ref, a1, a2, f1, f2, k1, k2, oa1, oa2, of1, of2,
    ok1, ok2, step_ref,
):
    clip = clip_ref[0]
    rows = wq0.shape[0]
    for k, grads in enumerate(((wq0, out0), (wq1, out1))):
        for i in range(2):
            one, two, step = moments_fast(grads[i][...] * clip, a1[0, k, i], a2[0, k, i])
            oa1[0, k, i] = one
            oa2[0, k, i] = two
            at = (2 * k + i) * rows
            for r in range(BLOCKS):
                step_ref[r, at : at + rows, :] = step[:, LANES * r : LANES * (r + 1)].astype(BF)
    cols = FF // BLOCKS // LANES
    for k, grads in enumerate((wide0, wide1)):
        for i in range(2):
            one, two, step = moments_fast(grads[i] * clip, f1[0, k, i], f2[0, k, i])
            of1[0, k, i] = one
            of2[0, k, i] = two
            for r in range(BLOCKS):
                for q in range(cols):
                    at = (2 * L + (2 * k + i) * cols + q) * rows
                    lane = LANES * (r * cols + q)
                    step_ref[r, at : at + rows, :] = step[:, lane : lane + LANES].astype(BF)
    one, two, step = moments_fast(kv_ref[...] * clip, k1[0], k2[0])
    ok1[0] = one
    ok2[0] = two
    at = (2 * L + 2 * L * cols) * rows
    for r in range(BLOCKS):
        moved = step if r == 0 else pltpu.roll(step, LANES - r * (LANES // BLOCKS), 1)
        step_ref[r, at : at + rows, :] = moved.astype(BF)


def settle(total, master, outer, rate, reps):
    mean_diff = rate * (total * (1.0 / reps) + DECAY * master)
    momentum = OUTER_MOMENTUM * outer + mean_diff
    return master - OUTER_RATE * (mean_diff + OUTER_MOMENTUM * momentum), momentum


def embed_settle_kernel(
    reps, rate, count_ref, at_ref, id_ref, extra_ref, base_ref, master_ref, outer_ref, *refs
):
    new_ref, mom_ref, scr = refs[-3:]
    tile = base_ref.shape[0]
    first = pl.program_id(0) * tile
    place = lax.broadcasted_iota(jnp.int32, (tile, 1), 0) + first
    scr[...] = base_ref[...].astype(F4)
    for g in range(reps):

        def add(i, part, g=g):
            hot = jnp.where(place == id_ref[g, i], 1.0, 0.0).astype(BF)
            scr[...] += nn(hot, extra_ref[g, part, :])

        overlapping(lambda k, g=g: at_ref[g, k], count_ref[g], first, tile, add)
    new_ref[0], mom_ref[0] = settle(scr[...], master_ref[0], outer_ref[0], rate, reps)


def embed_settle(reps, counts, ids, extra, base, master, outer, held):
    vr = base.shape[0]
    slots = extra.shape[1]
    whole = pl.BlockSpec((1, SETTLE, LANES), lambda i: (0, i, 0))
    return pl.pallas_call(
        partial(embed_settle_kernel, reps, LEARN_RATES[0]),
        grid=(pl.cdiv(vr, SETTLE),),
        in_specs=[
            SM,
            SM,
            pl.BlockSpec((reps, slots // GROUP, 1, GROUP), lambda i: (0, 0, 0, 0)),
            pl.BlockSpec((reps, slots, LANES), lambda i: (0, 0, 0)),
            pl.BlockSpec((SETTLE, LANES), lambda i: (i, 0)),
            whole,
            whole,
        ]
        + [ANY] * len(held),
        out_specs=[whole, whole],
        out_shape=[shaped(*master.shape)] * 2,
        input_output_aliases={7 + i: i for i in range(len(held))},
        scratch_shapes=[pltpu.VMEM((SETTLE, LANES), F4)],
        compiler_params=params(),
        name="embedding_settle",
        cost_estimate=takes(13),
    )(counts, ids.reshape(reps, -1), ids, extra, base, master, outer, *held)


def unembed_settle_kernel(reps, rate, sum_ref, master_ref, outer_ref, *refs):
    new_ref, mom_ref = refs[-2:]
    rows = sum_ref.shape[0]
    new_ref[0, :rows], mom_ref[0, :rows] = settle(
        sum_ref[...].astype(F4), master_ref[0, :rows], outer_ref[0, :rows], rate, reps
    )


def unembed_settle(reps, total, master, outer, held, piece, size):
    whole = pl.BlockSpec((1, size, LANES), lambda i: (1, piece, 0))
    return pl.pallas_call(
        partial(unembed_settle_kernel, reps, LEARN_RATES[0]),
        grid=(1,),
        in_specs=[pl.BlockSpec(total.shape, lambda i: (0, 0)), whole, whole] + [ANY] * len(held),
        out_specs=[whole, whole],
        out_shape=[shaped(*master.shape)] * 2,
        input_output_aliases={3 + i: i for i in range(len(held))},
        compiler_params=params(),
        name="unembedding_settle",
        cost_estimate=takes(3),
    )(total, master, outer, *held)


def body(
    token_ids,
    prompt_mask,
    loss_pos,
    tables,
    attention,
    feedforward,
    key_value,
    gains_biases,
    first_tables,
    first_attention,
    first_feedforward,
    first_key_value,
    first_gains,
    second_tables,
    second_attention,
    second_feedforward,
    second_key_value,
    second_gains,
    outer_tables,
    outer_attention,
    outer_feedforward,
    outer_key_value,
    outer_gains,
):
    width = lax.axis_size(WIDE_AXES)
    reps = lax.axis_size("rep")
    w = lax.axis_index(WIDE_AXES)
    rep = lax.axis_index("rep")
    seqs = token_ids.shape[3]
    rows_seq = LEN // width
    block = seqs * rows_seq
    cap = 2 * block // width
    vr = tables.shape[1]
    lrows = loss_pos.shape[4]
    n_micro = width * lrows
    n_loss = MICRO * n_micro
    span = width * cap
    n_slots = MICRO * span
    own_rows = D // width
    parity = w % 2

    def over_wide(value, k):
        return lax.ppermute(value, WIDE_AXES, [(i, i ^ k) for i in range(width)])

    def over_rep(value, k):
        return lax.ppermute(value, "rep", [(i, i ^ k) for i in range(reps)])

    def sum_wide(value, kind, beside=()):
        half = value.shape[0] // 2
        keep = lax.dynamic_slice_in_dim(value, parity * half, half)
        give = lax.dynamic_slice_in_dim(value, (1 - parity) * half, half)
        mine = (keep + over_wide(give, 1)).astype(kind)
        parts = [mine] + [over_wide(mine, k) for k in range(2, width, 2)]
        parts, *beside = lax.optimization_barrier((parts, *beside))
        parts = [part.astype(F4) for part in parts]
        while len(parts) > 1:
            parts = [parts[i] + parts[i + 1] for i in range(0, len(parts), 2)]
        total = parts[0].astype(value.dtype)
        other = over_wide(total, 1)
        joined = jnp.concatenate(
            [jnp.where(parity == 0, total, other), jnp.where(parity == 0, other, total)]
        )
        return (joined, *beside) if beside else joined

    scalars = jnp.stack(
        [
            w,
            parity,
            rep,
            w * vr,
            w * own_rows // LANES,
            w * own_rows % LANES,
            jnp.asarray(vr, jnp.int32),
            jnp.zeros((), jnp.int32),
        ]
    ).astype(jnp.int32)

    pack = jnp.concatenate(
        [feedforward[k, i] for k in range(L) for i in range(2)]
        + [attention[k, i] for k in range(L) for i in range(2)],
        axis=1,
    ).astype(BF)

    own_table = tables[1].astype(BF)

    n_mb = MICRO * width

    def by_block(array):
        array = array.reshape(MICRO, seqs, width, rows_seq).transpose(0, 2, 1, 3)
        return array.reshape(n_mb, block).astype(F4)

    tokens = by_block(token_ids)
    flat = jnp.concatenate([gains_biases, key_value.reshape(-1)])
    n_flat = flat.shape[0]
    n_small = gains_biases.shape[0]
    flat = jnp.pad(flat, (0, -n_flat % (8 * block))).reshape(-1, block)
    message = jnp.concatenate([tokens, flat])
    message, pack = lax.optimization_barrier((message, pack))
    pack_near = [over_wide(pack, k) for k in range(2, width, 2)]
    everyone = [message] + [over_rep(message, k) for k in range(1, reps)]
    lines = n_slots // LANES
    slot_ids, slot_codes, slot_rows, rest = call(
        partial(slots_kernel, seqs, rows_seq, vr, cap),
        [shaped(reps, lines, LANES, kind=jnp.int32)]
        + [shaped(lines, LANES, kind=jnp.int32)] * 2
        + [shaped(reps, *flat.shape)],
        (scalars, *everyone),
        scratch=[pltpu.VMEM((reps, *message.shape), F4)],
        smem=1,
        cost=7, name="slots",
    )
    (mine_w,) = call(
        stack_kernel,
        [shaped(width // 2, *pack.shape, kind=BF)],
        (pack, *pack_near),
        cost=2, name="stack_weights",
    )
    half_w = mine_w.shape[0] // 2
    x_w, y_w = over_rep(mine_w, 1), over_rep(mine_w, 2)
    slot_ids, mine_w = lax.optimization_barrier((slot_ids, mine_w))
    asked = [None] * reps
    for k in range(reps - 1, -1, -1):
        asked[k] = tables[0].at[slot_ids[k].reshape(-1)].get(mode="promise_in_bounds").astype(BF)
    rows = [asked[0]] + [over_rep(asked[k], k) for k in range(1, reps)]
    own_codes, own_ids = slot_codes.reshape(-1), slot_rows.reshape(-1)

    rest = rest.reshape(reps, -1)
    vectors, pair_bias, final_gain, final_bias = unpack_small(rest[:, :n_small].reshape(-1))
    final_rows = jnp.stack([final_gain, final_bias])
    vec = [vectors[k][None, :] for k in range(L)]
    kv_near = rest[:, n_small:n_flat].reshape(reps, own_rows, -1).transpose(1, 0, 2)
    kv_near = kv_near.reshape(own_rows, LANES).astype(BF)
    kv_near = [kv_near] + [over_wide(kv_near, k) for k in range(2, width, 2)]
    kv_near = [part for piece in kv_near for part in (piece, over_wide(piece, 1))]

    codes = loss_pos.reshape(n_mb, lrows)
    blocks = jnp.arange(n_mb, dtype=jnp.int32)[:, None]
    row_code = (
        blocks // width * (seqs * LEN)
        + codes // (rows_seq - 1) * LEN
        + blocks % width * rows_seq
        + codes % (rows_seq - 1)
    ).reshape(1, n_loss)
    frequency = 10000.0 ** (-2.0 * jnp.arange(ROT // 2, dtype=F4) / ROT)
    angles = jnp.concatenate([own_codes, row_code[0]]) % LEN
    angles = angles.astype(F4)[None, :] * frequency[:, None]
    turns = jnp.concatenate([jnp.cos(angles), jnp.sin(angles)])
    int_of = partial(shaped, kind=jnp.int32)
    (
        key_codes, chip_codes, slot_cols, row_cols, target_row, weight, slot_cos, slot_sin, row_cos,
        row_sin,
    ) = call(
        partial(places_kernel, seqs, rows_seq, vr, cap),
        [
            int_of(n_mb, 1, span), int_of(n_mb, 1, 2 * cap), int_of(n_slots, 2), int_of(n_loss, 2),
            int_of(1, n_loss), shaped(1, n_loss), shaped(n_slots, LANES), shaped(n_slots, LANES),
            shaped(n_loss, LANES), shaped(n_loss, LANES),
        ],
        (
            scalars, tokens, by_block(prompt_mask), loss_pos.reshape(-1, LANES), slot_codes, slot_rows,
            row_code, turns,
        ),
        smem=1,
        cost=4, name="places",
    )
    count = jnp.sum(weight)

    rows, x_w, y_w, kv_near, own_table = lax.optimization_barrier(
        (rows, x_w, y_w, kv_near, own_table)
    )

    unembed = lax.all_gather(own_table, "rep")
    d_w = [over_rep(x_w[:half_w], 2), over_rep(y_w[half_w:], 1)]
    pairs, stream, kv_low, rows = call(
        kv_kernel,
        [shaped(n_slots, LANES, kind=BF), shaped(BLOCKS, n_loss, LANES, kind=BF), shaped(D, LANES, kind=BF), shaped(reps, n_slots, LANES, kind=BF)],
        (
            scalars, *rows, slot_cos, slot_sin, vec[0], pair_bias[None, :], own_codes[None, :],
            row_cols, *kv_near,
        ),
        smem=1,
        cost=2, name="keys_values",
    )
    keep = lax.dynamic_slice_in_dim(stream, 2 * parity, 2)
    give = lax.dynamic_slice_in_dim(stream, 2 * (1 - parity), 2)
    keep = (keep + over_wide(give, 1)).reshape(2 * n_loss, LANES)
    near = jnp.concatenate([pairs, keep])
    near = [near] + [over_wide(near, k) for k in range(2, width, 2)]
    base_step = base_pass(first_tables, second_tables, pairs)
    near, base_step, d_w = lax.optimization_barrier((near, base_step, d_w))
    pieces = []
    for piece in near:
        pieces += [piece, over_wide(piece, 1)]
    weights = [mine_w, x_w, y_w, *d_w]
    weights = weights + [over_wide(part, 1) for part in weights]


    keys, stream = call(
        partial(order_kernel, seqs, rows_seq, width, cap),
        [shaped(MICRO * width, block, LANES, kind=BF), shaped(BLOCKS, n_loss, LANES)],
        (scalars, base_step, key_codes, *pieces),
        smem=1,
        far=(1,),
        cost=5, name="token_order",
    )
    weights = [mine_w, x_w, y_w, *d_w]
    weights = weights + [over_wide(part, 1) for part in weights]

    tiles = width // SPREAD
    keys = keys.reshape(MICRO, tiles, SPREAD * block, LANES)

    codes = (row_cols,)
    halves = shaped(2, n_loss, LANES)
    att_room = [pltpu.VMEM((reps, D, ATT), BF), pltpu.SemaphoreType.DMA((2, 4, width // 2))]
    ff_room = [pltpu.VMEM((reps, D, WIDE), BF), pltpu.SemaphoreType.DMA((2, 4, width // 2))]
    both_room = [att_room[0], ff_room[0], pltpu.SemaphoreType.DMA((2, 2, 4, width // 2))]
    stacked = ROWS * HEADS // 2
    logs = shaped(n_loss // ROWS, stacked, 1)
    scores = pltpu.VMEM((tiles, stacked, SPREAD * block), F4)
    whole = shaped(n_loss, D)

    def other_half(value):
        return over_wide(value.astype(BF), 1)

    stream0, q0, ctx0, log0 = call(
        partial(first_kernel, seqs, rows_seq),
        [whole, halves, halves, logs],
        (scalars, stream, vec[0], *weights, keys, *codes, row_cos, row_sin),
        smem=1,
        scratch=[scores] + att_room,
        far=range(3, 13),
        cost=9, name="first_attention",
    )
    far0 = other_half(ctx0)
    (partial0,) = call(partial(feed_kernel, 0), [whole], (scalars, stream0, vec[0], *weights), smem=1, scratch=ff_room, far=range(3, 13), name="first_feed")
    partial0, unembed = lax.optimization_barrier((partial0, unembed))
    stream1, q1, ctx1, log1 = call(
        partial(second_kernel, seqs, rows_seq),
        [whole, halves, halves, logs],
        (scalars, partial0, ctx0, far0, vec[1], *weights, keys, *codes, row_cos, row_sin),
        smem=1,
        scratch=[scores] + att_room,
        far=range(5, 15),
        cost=9, name="second_attention",
    )
    far1 = other_half(ctx1)

    (partial1,) = call(partial(feed_kernel, 1), [whole], (scalars, stream1, vec[1], *weights), smem=1, scratch=ff_room, far=range(3, 13), name="second_feed")
    logits, stats, stream2, picked = call(
        logits_kernel,
        [shaped(vr, n_loss), shaped(8, n_loss), whole, shaped(n_loss, D, kind=BF)],
        (scalars, partial1, ctx1, far1, *weights, final_rows, target_row, unembed),
        smem=1,
        scratch=att_room,
        far=range(4, 14),
        cost=10, name="logits",
    )
    near = [stats] + [over_wide(stats, k) for k in range(2, width, 2)]
    stats = jnp.stack([part for piece in near for part in (piece, over_wide(piece, 1))])
    probs, grad_picked, loss_sum = call(
        probs_kernel,
        [shaped(vr, n_loss, kind=BF), shaped(BLOCKS, n_loss, LANES), shaped(1, 1)],
        (scalars, stats, weight, target_row, logits, unembed),
        smem=1,
        out_specs=[VM, VM, SM],
        cost=9, name="loss_gradient",
    )
    base_step, grad_picked = lax.optimization_barrier((base_step, grad_picked))
    base_sum = lax.psum_scatter(base_step, "rep", scatter_dimension=0, tiled=True)[0]

    (unembed_square,) = call(
        squares_kernel, [shaped(1, 1)], (probs, picked), out_specs=[SM], cost=3, name="squares"
    )
    grad_picked, unembed_square = sum_wide(grad_picked, BF, (unembed_square,))

    wide_shape = shaped(2, own_rows, FF)
    out_shape = shaped(own_rows, D)
    vec_shape = shaped(1, 7 * D + FF)
    head_shape = shaped(1, 3 * D)
    dq_shape = shaped(2, n_loss, LANES, kind=BF)
    dkv_shape = shaped(MICRO, tiles, SPREAD * block, LANES)
    slots_shape = shaped(n_slots, LANES)
    pull_scratch = [
        pltpu.VMEM((BLOCKS, n_loss, LANES), BF),
        pltpu.VMEM((BLOCKS, n_loss, LANES), BF),
        pltpu.VMEM((2, n_loss, LANES), F4),
        pltpu.VMEM((LANES, D), F4),
    ]
    dq1, dkv, wide1, out1, vec1, final_grad, grad_stream, grad_feed, square1 = call(
        partial(last_pull_kernel, seqs, rows_seq),
        [
            dq_shape, dkv_shape, wide_shape, out_shape, vec_shape, shaped(2, D), whole, whole,
            shaped(1, 1),
        ],
        (
            scalars, unembed_square, grad_picked, final_rows, stream2, stream1, vec[1], *weights, ctx1,
            far1, q1, log1, keys, *codes,
        ),
        smem=2,
        out_specs=[VM] * 8 + [SM],
        scratch=pull_scratch + both_room,
        far=range(7, 17),
        cost=16, name="second_pull",
    )
    far_dq1 = over_wide(dq1, 1)
    dq0, own_dkv, near_dkv, wide0, out0, vec0, wq1, head1, grad_stream, grad_feed, square0 = call(
        partial(first_pull_kernel, seqs, rows_seq),
        [
            dq_shape, slots_shape, slots_shape, wide_shape, out_shape, vec_shape, out_shape,
            head_shape, whole, whole, shaped(1, 1),
        ],
        (
            scalars, grad_stream, grad_feed, dq1, far_dq1, stream1, vec[1], stream0, vec[0],
            *weights, ctx0, far0, q0, log0, keys, *codes, row_cos, row_sin, dkv,
            chip_codes,
        ),
        smem=1,
        out_specs=[VM] * 10 + [SM],
        scratch=pull_scratch
        + [pltpu.VMEM(dkv_shape.shape, F4)]
        + both_room
        + [pltpu.SemaphoreType.DMA],
        far=[*range(9, 19), 27],
        cost=23, name="first_pull",
    )
    far_dq0 = over_wide(dq0, 1)
    far_dkv = over_wide(near_dkv, 1)
    wq0, head0, grad_rows, row_ids, kv_part, gain_part, square_rows, row_count = call(
        embed_pull_kernel,
        [
            out_shape, head_shape, shaped(n_slots, D, kind=BF), shaped(n_slots, 1, kind=jnp.int32),
            shaped(D, LANES), shaped(8, D), shaped(1, 1), shaped(1, 1, kind=jnp.int32),
        ],
        (
            scalars, grad_stream, grad_feed, dq0, far_dq0, stream0, vec[0], *weights, kv_low, row_cos,
            row_sin, own_dkv, far_dkv, rows, slot_cos, slot_sin,
            slot_cols, row_code, own_ids[None, :],
        ),
        smem=1,
        out_specs=[VM] * 6 + [SM, SM],
        scratch=[
            pltpu.VMEM((BLOCKS, n_loss, LANES), BF),
            pltpu.VMEM((LANES, D), F4),
            pltpu.VMEM((n_slots, D), BF),
            pltpu.VMEM((n_slots, D), BF),
        ]
        + att_room,
        far=range(7, 17),
        cost=12, name="embedding_pull",
    )

    square = (square0 + square1 + square_rows)[0, 0]
    message = jnp.concatenate(
        [kv_part, gain_part.reshape(-1, LANES), jnp.full((16, LANES), square, F4)]
    )
    message, base_sum = sum_wide(message, F4, (base_sum,))
    kv_total = message[:D]
    gain_total = message[D : D + 8 * BLOCKS].reshape(8, D)
    square = message[D + 8 * BLOCKS, 0]

    def vector_grad(head, vec_part):
        return [head[0, : 2 * D], vec_part[0, 2 * D : 4 * D], head[0, 2 * D :], vec_part[0, 5 * D :]]

    grad_small = jnp.concatenate(
        [head0[0, : 2 * D] + gain_total[:2].reshape(-1)]
        + vector_grad(head0, vec0)[1:]
        + vector_grad(head1, vec1)
        + [gain_total[2, :LANES], final_grad.reshape(-1)]
    )
    square = square + jnp.sum(kv_total * kv_total) + jnp.sum(grad_small * grad_small)
    clip_factor = jnp.minimum(1.0, CLIP / (jnp.sqrt(square) + 1e-06))

    clip = clip_factor.reshape(1)

    n_tiles = pl.cdiv(vr, TILE)
    size = n_tiles
    pieces = pl.cdiv(n_tiles, size)
    bounds = [min(size * i, n_tiles) for i in range(pieces + 1)]
    held = []
    terms = []

    for i in range(pieces):
        *held, step = unembed_pass(
            clip, probs, picked, first_tables, second_tables, held, bounds[i],
            bounds[i + 1] - bounds[i],
        )
        terms.append(lax.psum_scatter(step, "rep", scatter_dimension=0, tiled=True)[0])

    kv_grad = lax.dynamic_slice_in_dim(kv_total, w * own_rows, own_rows, axis=0)
    sm_one, sm_two, sm_step = moments_step(
        grad_small * clip_factor, first_gains[0], second_gains[0]
    )
    pack_rows = own_rows * (2 * L + 2 * L * (FF // BLOCKS // LANES) + 1)
    att_one, att_two, ff_one, ff_two, kv_one, kv_two, packed = call(
        layers_kernel,
        [shaped(*first_attention.shape)] * 2
        + [shaped(*first_feedforward.shape)] * 2
        + [shaped(*first_key_value.shape)] * 2
        + [shaped(BLOCKS, pack_rows, LANES, kind=BF)],
        (
            clip, step, wq0, out0, wq1, out1, wide0, wide1, kv_grad, first_attention, second_attention,
            first_feedforward, second_feedforward, first_key_value, second_key_value,
        ),
        smem=1,
        far=(1,),
        cost=8, name="layers_adam",
    )
    n_small = sm_step.shape[0] // reps
    sm_step = jnp.pad(sm_step.astype(BF).reshape(reps, n_small), ((0, 0), (0, -n_small % 2048)))
    packed = jnp.concatenate([packed, sm_step.reshape(reps, -1, LANES)], axis=1)
    steps = packed
    packed = lax.all_to_all(packed, "rep", 0, 0, tiled=True)
    packed = jnp.sum(packed.astype(F4), axis=0)

    e_tiles = pl.cdiv(vr, TILE)
    e_pieces = min(2, e_tiles)
    e_bounds = [e_tiles * i // e_pieces for i in range(e_pieces + 1)]
    extra = 0.0
    for i in range(e_pieces):
        *held, part = embed_pass(
            clip, row_count.reshape(1), row_ids, grad_rows, first_tables, second_tables, base_step, held,
            steps, e_bounds[i], e_bounds[i + 1] - e_bounds[i],
        )
        extra = extra + part
    one_tables, two_tables = held
    coded = jnp.concatenate([(row_ids + LANES) // LANES, (row_ids + LANES) % LANES])
    coded = jnp.broadcast_to(coded.astype(BF).reshape(1, -1, LANES), (reps, n_slots // 64, LANES))
    extra = jnp.concatenate([extra.astype(BF), coded], axis=1)
    extra = lax.all_to_all(extra, "rep", 0, 0, tiled=True)
    coded = extra[:, n_slots:].reshape(reps, 2, n_slots).astype(jnp.int32)
    coded = coded[:, 0] * LANES + coded[:, 1] - LANES
    counts = jnp.sum((coded >= 0).astype(jnp.int32), axis=1)

    new_tables = ()
    for i in range(pieces - 1):
        new_tables = unembed_settle(
            reps, terms[i], tables, outer_tables, new_tables, i, terms[0].shape[0]
        )
    new_tables = embed_settle(
        reps, counts, coded.reshape(reps, n_slots // GROUP, 1, GROUP), extra, base_sum, tables,
        outer_tables, new_tables,
    )
    new_tables = unembed_settle(
        reps, terms[-1], tables, outer_tables, new_tables, pieces - 1, terms[0].shape[0]
    )

    cols = FF // BLOCKS // LANES
    at_ff = 2 * L * own_rows
    at_kv = at_ff + 2 * L * cols * own_rows
    masters = (attention, feedforward, key_value, gains_biases)
    outers = (outer_attention, outer_feedforward, outer_key_value, outer_gains)
    sums = (
        packed[:at_ff].reshape(L, 2, own_rows, LANES),
        packed[at_ff:at_kv]
        .reshape(L, 2, cols, own_rows, LANES)
        .transpose(0, 1, 3, 2, 4)
        .reshape(feedforward.shape),
        packed[at_kv : at_kv + own_rows, : LANES // BLOCKS],
        packed[pack_rows:].reshape(-1)[:n_small],
    )
    stepped = [new_tables] + [
        settle(sums[i], masters[i], outers[i], LEARN_RATES[i + 1], reps) for i in range(4)
    ]
    return (
        loss_sum.reshape(1),
        count.reshape(1),
        *[pair[0] for pair in stepped],
        one_tables,
        att_one,
        ff_one,
        kv_one,
        sm_one[None],
        two_tables,
        att_two,
        ff_two,
        kv_two,
        sm_two[None],
        *[pair[1] for pair in stepped],
    )


def solution(mesh):
    split = (
        P(None, WIDE_AXES, "rep"),
        P(None, None, WIDE_AXES, "rep"),
        P(None, None, WIDE_AXES, "rep"),
        P(WIDE_AXES, "rep"),
        P("rep"),
    )
    moments = (
        P("rep", None, WIDE_AXES, None),
        P("rep", None, None, WIDE_AXES, None),
        P("rep", None, None, WIDE_AXES, None),
        P("rep", WIDE_AXES, None),
        P("rep", None),
    )
    tokens = P("rep", None, None, None, None)
    parted = mesh.devices.reshape(mesh.shape["rep"], mesh.shape["wide"] // 2, 2)
    return jax.shard_map(
        body,
        mesh=Mesh(parted, ("rep",) + WIDE_AXES),
        in_specs=(tokens,) * 3 + split + moments + moments + split,
        out_specs=(P("rep"), P("rep")) + split + moments + moments + split,
        check_vma=False,
    )
```

profile of v0, /device:TPU:0, one launch (start us, length us, event | category | flops | bytes accessed | tf_op | source)
XLA Modules:
  0.0 490.8 jit_solution(7552361788715868862)
XLA Ops:
  11.9 3.0 collective-permute-start
  18.5 2.6 collective-permute-start.4
  21.1 5.0 %fusion = (bf16[6288,128]{1,0:T(8,128)(2,1)}, bf16[6288,128]{1,0:T(8,128)(2,1)}) fusion(f32[2,6288,128]{2,1,0:T(8,128)} %master_ref.3), kind=kLoop, calls=%fused_computation.8 | loop fusion | bytes 6438912 | tf_op jit(solution)/shard_map/convert_element_type | solution.py:1276
  27.3 7.6 %slots.1 = (s32[4,8,128]{2,1,0:T(8,128)}, s32[8,128]{1,0:T(8,128)}, s32[8,128]{1,0:T(8,128)}, f32[4,24,256]{2,1,0:T(8,128)}) custom-call(s32[8]{0:T(128)} %stack.63.sc_ref, f32[40,256]{1,0:T(8,128)} %copy-done.27, f32[40,256]{1,0:T(8,128)} %copy-done.40, f32[40,256]{1,0:T(8,128)} %copy-done.41, f32[40,256]{1,0:T(8,128)} %collective-permute-done.2.d_all), custom_call_target="tpu_custom_call" | custom-call | bytes 21000000 | tf_op jit(solution)/shard_map/slots/pallas_call | solution.py:116
  38.4 3.5 collective-permute-start.14
  41.9 2.5 collective-permute-done.4.refs_2_
  45.1 2.4 stack_weights.1.w0
  54.7 2.8 collective-permute-done.16.refs_6_
  57.8 4.3 gather_fusion.1
  62.1 4.3 gather_fusion.2
  66.4 3.2 gather_fusion.3
  70.8 2.4 collective-permute-start.8
  73.5 4.3 gather_fusion
  77.8 6.5 %collective-permute-done.6.r1 = bf16[1024,128]{1,0:T(8,128)(2,1)S(1)} collective-permute-done((bf16[1024,128]{1,0:T(8,128)(2,1)}, bf16[1024,128]{1,0:T(8,128)(2,1)S(1)}, u32[]{:S(2)}, u32[]{:S(2)}) %collective-permute-start.6) | collective-permute-done | bytes 262176 | tf_op jit(solution)/shard_map/ppermute | solution.py:1238
  84.3 4.0 collective-permute-done.7.r2
  93.8 3.7 places.1
  98.7 4.4 keys_values.1
  111.1 5.0 %collective-permute-start.19 = (bf16[1536,128]{1,0:T(8,128)(2,1)}, bf16[1536,128]{1,0:T(8,128)(2,1)}, u32[]{:S(2)}, u32[]{:S(2)}) collective-permute-start(bf16[1536,128]{1,0:T(8,128)(2,1)} %pad_maximum_fusion.2.refs_0_), channel_id=1, source_target_pairs={{0,2},{1,3},{2,0},{3,1},{4,6},{5,7},{6,4},{7,5},{8,10},{9,11},{10,... | collective-permute-start | bytes 1179656 | tf_op jit(solution)/shard_map/ppermute | solution.py:1235
  118.5 13.7 %embedding_base.1.after_ref.base_ref = bf16[4,6288,128]{2,1,0:T(8,128)(2,1)} custom-call(f32[1,2,6288,512]{3,2,1,0:T(8,128)} %first_ref.7, f32[1,2,6288,512]{3,2,1,0:T(8,128)} %second_ref.7, bf16[1024,128]{1,0:T(8,128)(2,1)} %get-tuple-element.167.after_ref), custom_call_target="tpu_custom_call" | custom-call | bytes 42000000 | tf_op jit(solution)/shard_map/embedding_base/pallas_call | solution.py:954
  133.3 12.9 %collective-permute-done.20.refs_4_ = bf16[1536,128]{1,0:T(8,128)(2,1)} collective-permute-done((bf16[1536,128]{1,0:T(8,128)(2,1)}, bf16[1536,128]{1,0:T(8,128)(2,1)}, u32[]{:S(2)}, u32[]{:S(2)}) %collective-permute-start.20) | collective-permute-done | bytes 393248 | tf_op jit(solution)/shard_map/ppermute | solution.py:1235
  149.5 2.3 collective-permute-done.26.refs_5_
  153.8 6.6 %token_order.1 = (bf16[16,256,128]{2,1,0:T(8,128)(2,1)}, f32[4,256,128]{2,1,0:T(8,128)}) custom-call(s32[8]{0:T(128)} %stack.63.sc_ref, bf16[4,6288,128]{2,1,0:T(8,128)(2,1)} %embedding_base.1.after_ref.base_ref, s32[16,1,512]{2,1,0:T(1,128)} %get-tuple-element.172.code_ref, bf16[1536,128]{1,0:T(8,128)(2,1)} %pad_maximum_fusion.2.refs_0_, ...), custom_call_target="tpu_custom_call" | custom-call | bytes 15000000 | tf_op jit(solution)/shard_map/token_order/pallas_call | solution.py:116
  160.4 11.4 %first_attention.1 = (f32[256,512]{1,0:T(8,128)}, f32[2,256,128]{2,1,0:T(8,128)}, f32[2,256,128]{2,1,0:T(8,128)}, f32[4,256,1]{2,1,0:T(8,128)}) custom-call(s32[8]{0:T(128)} %stack.63.sc_ref, f32[4,256,128]{2,1,0:T(8,128)} %get-tuple-element.177.low_ref, f32[1,5632]{1,0:T(1,128)} %slice.177.vec_ref, bf16[4,64,2560]{2,1,0:T(8,128)(2,1)} %stack_weights.1.w0, ...), custom_call_target="tpu_custom_call" | custom-call | bytes 27000000 | tf_op jit(solution)/shard_map/first_attention/pallas_call | solution.py:116
  173.9 6.1 %first_feed.1.partial_ref = f32[256,512]{1,0:T(8,128)} custom-call(s32[8]{0:T(128)} %stack.63.sc_ref, f32[256,512]{1,0:T(8,128)} %get-tuple-element.184.stream_ref, f32[1,5632]{1,0:T(1,128)} %slice.177.vec_ref, bf16[4,64,2560]{2,1,0:T(8,128)(2,1)} %stack_weights.1.w0, bf16[4,64,2560]{2,1,0:T(8,128)(2,1)} %collective-permute-done.9.w1, ...), custom_call_target="tpu_custom_call" | custom-call | bytes 15000000 | tf_op jit(solution)/shard_map/first_feed/pallas_call | solution.py:116
  180.7 11.7 %second_attention.1 = (f32[256,512]{1,0:T(8,128)}, f32[2,256,128]{2,1,0:T(8,128)}, f32[2,256,128]{2,1,0:T(8,128)}, f32[4,256,1]{2,1,0:T(8,128)}) custom-call(s32[8]{0:T(128)} %stack.63.sc_ref, f32[256,512]{1,0:T(8,128)} %first_feed.1.partial_ref, f32[2,256,128]{2,1,0:T(8,128)} %get-tuple-element.187.own_ref, bf16[2,256,128]{2,1,0:T(8,128)(2,1)} %copy-done.6, ...), custom_call_target="tpu_custom_call" | custom-call | bytes 27000000 | tf_op jit(solution)/shard_map/second_attention/pallas_call | solution.py:116
  194.2 6.1 %second_feed.1.partial_ref = f32[256,512]{1,0:T(8,128)} custom-call(s32[8]{0:T(128)} %stack.63.sc_ref, f32[256,512]{1,0:T(8,128)} %get-tuple-element.188.stream_ref.stream1_ref, f32[1,5632]{1,0:T(1,128)} %slice.182.vec_ref.vec1_ref, bf16[4,64,2560]{2,1,0:T(8,128)(2,1)} %stack_weights.1.w0, bf16[4,64,2560]{2,1,0:T(8,128)(2,1)} %collective-permute-done.9.w1, ...), custom_call_target="tpu_custom_call" | custom-call | bytes 15000000 | tf_op jit(solution)/shard_map/second_feed/pallas_call | solution.py:116
  200.9 10.7 %logits.1 = (f32[6288,256]{1,0:T(8,128)}, f32[8,256]{1,0:T(8,128)}, f32[256,512]{1,0:T(8,128)}, bf16[256,512]{1,0:T(8,128)(2,1)}) custom-call(s32[8]{0:T(128)} %stack.63.sc_ref, f32[256,512]{1,0:T(8,128)} %second_feed.1.partial_ref, f32[2,256,128]{2,1,0:T(8,128)} %get-tuple-element.189.own_ref, bf16[2,256,128]{2,1,0:T(8,128)(2,1)} %copy-done.7, ...), custom_call_target="tpu_custom_call" | custom-call | bytes 30000000 | tf_op jit(solution)/shard_map/logits/pallas_call | solution.py:116
  212.1 7.7 %collective-permute-start.36 = (f32[8,256]{1,0:T(8,128)}, f32[8,256]{1,0:T(8,128)S(1)}, u32[]{:S(2)}, u32[]{:S(2)}) collective-permute-start(f32[8,256]{1,0:T(8,128)} %get-tuple-element.192), channel_id=1, source_target_pairs={{0,2},{1,3},{2,0},{3,1},{4,6},{5,7},{6,4},{7,5},{8,10},{9,11},{10,... | collective-permute-start | bytes 24584 | tf_op jit(solution)/shard_map/ppermute | solution.py:1235
  223.0 2.3 collective-permute-done.38
  229.0 8.8 %loss_gradient.1 = (bf16[6288,256]{1,0:T(8,128)(2,1)}, f32[4,256,128]{2,1,0:T(8,128)}, f32[1,1]{1,0:T(1,128)}) custom-call(s32[8]{0:T(128)} %stack.63.sc_ref, f32[8,8,256]{2,1,0:T(8,128)} %copy-done.34, f32[1,256]{1,0:T(1,128)} %get-tuple-element.193.weight_ref, s32[1,256]{1,0:T(1,128)} %get-tuple-element.190.target_ref, ...), custom_call_target="tpu_custom_call" | custom-call | bytes 27000000 | tf_op jit(solution)/shard_map/loss_gradient/pallas_call | solution.py:116
  242.6 2.4 collective-permute-start.45
  245.0 5.0 %squares.1.before_ref = f32[1,1]{1,0:T(1,128)} custom-call(bf16[6288,256]{1,0:T(8,128)(2,1)} %get-tuple-element.198.probs_ref, bf16[256,512]{1,0:T(8,128)(2,1)} %get-tuple-element.199.picked_ref), custom_call_target="tpu_custom_call" | custom-call | bytes 9000000 | tf_op jit(solution)/shard_map/squares/pallas_call | solution.py:116
  250.0 3.8 collective-permute-done.44
  256.3 17.2 %second_pull.1 = (bf16[2,256,128]{2,1,0:T(8,128)(2,1)}, f32[2,2,1024,128]{3,2,1,0:T(8,128)}, f32[2,64,2048]{2,1,0:T(8,128)}, f32[64,512]{1,0:T(8,128)}, f32[1,56...) custom-call(s32[8]{0:T(128)} %stack.63.sc_ref, ...), custom_call_target="tpu_custom_call" | custom-call | bytes 48000000 | tf_op jit(solution)/shard_map/second_pull/pallas_call | solution.py:116
  275.8 23.2 %first_pull.1 = (bf16[2,256,128]{2,1,0:T(8,128)(2,1)}, f32[1024,128]{1,0:T(8,128)}, f32[1024,128]{1,0:T(8,128)}, f32[2,64,2048]{2,1,0:T(8,128)}, f32[64,512]{1,0...) custom-call(s32[8]{0:T(128)} %stack.63.sc_ref, ...), custom_call_target="tpu_custom_call" | custom-call | bytes 69000000 | tf_op jit(solution)/shard_map/first_pull/pallas_call | solution.py:116
  302.2 12.4 %embedding_pull.1 = (f32[64,512]{1,0:T(8,128)}, f32[1,1536]{1,0:T(1,128)}, bf16[1024,512]{1,0:T(8,128)(2,1)}, s32[1024,1]{1,0:T(8,128)}, f32[512,128]{1,0:T(8,12...) custom-call(s32[8]{0:T(128)} %stack.63.sc_ref, f32[256,512]{1,0:T(8,128)} %get-tuple-element.215.grad_in_ref, ...), custom_call_target="tpu_custom_call" | custom-call | bytes 36000000 | tf_op jit(solution)/shard_map/embedding_pull/pallas_call | solution.py:116
  323.4 3.6 collective-permute-done.51
  327.0 7.7 %collective-permute-done.52 = f32[280,128]{1,0:T(8,128)S(1)} collective-permute-done((f32[280,128]{1,0:T(8,128)S(1)}, f32[280,128]{1,0:T(8,128)S(1)}, u32[]{:S(2)}, u32[]{:S(2)}) %collective-permute-start.52) | collective-permute-done | bytes 143392 | tf_op jit(solution)/shard_map/ppermute | solution.py:1235
  340.3 27.5 %unembedding_adam.1 = (f32[1,2,6288,512]{3,2,1,0:T(8,128)}, f32[1,2,6288,512]{3,2,1,0:T(8,128)}, bf16[4,6288,128]{2,1,0:T(8,128)(2,1)}) custom-call(f32[1]{0:T(128)} %bitcast.55.clip_ref, bf16[6288,256]{1,0:T(8,128)(2,1)} %get-tuple-element.198.probs_ref, bf16[256,512]{1,0:T(8,128)(2,1)} %get-tuple-element.199.picked_ref, f32[1,2,6288,512]{3,2,1,0:T(8,128)} %first_ref.7, ...), custom_call_target="tpu_custom_call" | custom-call | bytes 48000000 | tf_op jit(solution)/shard_map/unembedding_adam/pallas_call | solution.py:980
  372.3 9.1 %layers_adam.1 = (f32[1,2,2,64,512]{4,3,2,1,0:T(8,128)}, f32[1,2,2,64,512]{4,3,2,1,0:T(8,128)}, f32[1,2,2,64,2048]{4,3,2,1,0:T(8,128)}, f32[1,2,2,64,2048]{4,3,2...) custom-call(f32[1]{0:T(128)} %bitcast.55.clip_ref, ...), custom_call_target="tpu_custom_call" | custom-call | bytes 24000000 | tf_op jit(solution)/shard_map/layers_adam/pallas_call | solution.py:116
  381.5 2.7 constant_dynamic-update-slice_fusion.14
  384.8 19.1 %embedding_adam.2 = (f32[1,2,6288,512]{3,2,1,0:T(8,128)}, f32[1,2,6288,512]{3,2,1,0:T(8,128)}, f32[4,1024,128]{2,1,0:T(8,128)}) custom-call(f32[1]{0:T(128)} %bitcast.55.clip_ref, s32[1]{0:T(128)} %bitcast.57.count_ref, s32[1024]{0:T(1024)} %get-tuple-element.346.at_ref, s32[8,1,128]{2,1,0:T(1,128)} %bitcast.164, ...), custom_call_target="tpu_custom_call", output_to_operand_aliasing={{0}: (9, {}), {1}: (10, {})} | custom-call | bytes 51000000 | tf_op jit(solution)/shard_map/embedding_adam/pallas_call | solution.py:1059
  403.9 17.6 %embedding_adam.3 = (f32[1,2,6288,512]{3,2,1,0:T(8,128)}, f32[1,2,6288,512]{3,2,1,0:T(8,128)}, f32[4,1024,128]{2,1,0:T(8,128)}) custom-call(f32[1]{0:T(128)} %bitcast.55.clip_ref, s32[1]{0:T(128)} %bitcast.57.count_ref, s32[1024]{0:T(1024)} %get-tuple-element.346.at_ref, s32[8,1,128]{2,1,0:T(1,128)} %bitcast.165, ...), custom_call_target="tpu_custom_call", output_to_operand_aliasing={{0}: (9, {}), {1}: (10, {})} | custom-call | bytes 51000000 | tf_op jit(solution)/shard_map/embedding_adam/pallas_call | solution.py:1059
  421.5 2.4 add_convert_fusion
  424.0 25.4 %all_to_all.10.extra_ref = bf16[4,1040,128]{2,1,0:T(8,128)(2,1)S(1)} all-to-all(bf16[4,1040,128]{2,1,0:T(8,128)(2,1)S(1)} %pad_maximum_fusion), channel_id=1, replica_groups=mesh['rep'=4,'chip'=4,'core'=2] {'rep'}, dimensions={0} | all-to-all | bytes 2129920 | tf_op jit(solution)/shard_map/all_to_all | solution.py:1621
  449.4 4.6 all-to-all-start.1
  456.1 13.9 %embedding_settle.1 = (f32[2,6288,128]{2,1,0:T(8,128)}, f32[2,6288,128]{2,1,0:T(8,128)}) custom-call(s32[4]{0:T(128)} %get-tuple-element.342.count_ref, s32[4,1024]{1,0:T(4,128)} %bitcast.163, s32[4,8,1,128]{3,2,1,0:T(1,128)} %sub.56.id_ref, bf16[4,1040,128]{2,1,0:T(8,128)(2,1)} %copy-done.3, bf16[6288,128]{1,0:T(8,128)(2,1)} %bitcast.154, ...), custom_call_target="tpu_custom_call" | custom-call | bytes 39000000 | tf_op jit(solution)/shard_map/embedding_settle/pallas_call | solution.py:1146
  476.5 7.3 %unembedding_settle.1 = (f32[2,6288,128]{2,1,0:T(8,128)}, f32[2,6288,128]{2,1,0:T(8,128)}) custom-call(bf16[6288,128]{1,0:T(8,128)(2,1)} %bitcast.155, f32[2,6288,128]{2,1,0:T(8,128)} %master_ref.3, f32[2,6288,128]{2,1,0:T(8,128)} %outer_ref.3, f32[2,6288,128]{2,1,0:T(8,128)} %get-tuple-element.256.refs_0_, ...), custom_call_target="tpu_custom_call", output_to_operand_aliasing={{0}: (3, {}), {1}: (4, {})} | custom-call | bytes 9000000 | tf_op jit(solution)/shard_map/unembedding_settle/pallas_call | solution.py:1179
  (374 shorter events, 94.5 us)
Async XLA Ops:
  7.2 172.8 %all-gather.3.cloned.1.call-start = ((), (), s32[]{:S(2)}) async-start(), calls=%async_computation.4 | async-start | bytes 8048640 | tf_op jit(solution)/shard_map/all_gather | solution.py:1364
  11.9 9.2 %collective-permute-start = (f32[40,256]{1,0:T(8,128)S(1)}, f32[40,256]{1,0:T(8,128)S(1)}, u32[]{:S(2)}, u32[]{:S(2)}) collective-permute-start(f32[40,256]{1,0:T(8,128)S(1)} %pad_maximum_fusion.5.own_all), channel_id=1, source_target_pairs={{0,8},{8,0},{16,24},{24,16},{1,9},{9,1},{17,25},{25,17},{2,10},{10... | collective-permute-start | bytes 122888 | tf_op jit(solution)/shard_map/ppermute | solution.py:1238
  14.9 11.8 %collective-permute-start.1 = (f32[40,256]{1,0:T(8,128)S(1)}, f32[40,256]{1,0:T(8,128)S(1)}, u32[]{:S(2)}, u32[]{:S(2)}) collective-permute-start(f32[40,256]{1,0:T(8,128)S(1)} %pad_maximum_fusion.5.own_all), channel_id=1, source_target_pairs={{0,16},{8,24},{16,0},{24,8},{1,17},{9,25},{17,1},{25,9},{2,18},{10... | collective-permute-start | bytes 122888 | tf_op jit(solution)/shard_map/ppermute | solution.py:1238
  16.4 10.9 %collective-permute-start.2 = (f32[40,256]{1,0:T(8,128)S(1)}, f32[40,256]{1,0:T(8,128)}, u32[]{:S(2)}, u32[]{:S(2)}) collective-permute-start(f32[40,256]{1,0:T(8,128)S(1)} %pad_maximum_fusion.5.own_all), channel_id=1, source_target_pairs={{0,24},{8,16},{16,8},{24,0},{1,25},{9,17},{17,9},{25,1},{2,26},{10... | collective-permute-start | bytes 122888 | tf_op jit(solution)/shard_map/ppermute | solution.py:1238
  16.4 22.0 %collective-permute-start.3 = (bf16[64,2560]{1,0:T(8,128)(2,1)S(1)}, bf16[64,2560]{1,0:T(8,128)(2,1)S(1)}, u32[]{:S(2)}, u32[]{:S(2)}) collective-permute-start(bf16[64,2560]{1,0:T(8,128)(2,1)S(1)} %constant_dynamic-update-slice_fusion.refs_0_), channel_id=1, source_target_pairs={{0,2},{1,3},{2,0},{3,1},{4,6},{5,7},{6,4},{7,5},{8,10},{9,11},{10,... | collective-permute-start | bytes 983048 | tf_op jit(solution)/shard_map/ppermute | solution.py:1235
  18.5 25.9 %collective-permute-start.4 = (bf16[64,2560]{1,0:T(8,128)(2,1)S(1)}, bf16[64,2560]{1,0:T(8,128)(2,1)S(1)}, u32[]{:S(2)}, u32[]{:S(2)}) collective-permute-start(bf16[64,2560]{1,0:T(8,128)(2,1)S(1)} %constant_dynamic-update-slice_fusion.refs_0_), channel_id=1, source_target_pairs={{0,4},{1,5},{2,6},{3,7},{4,0},{5,1},{6,2},{7,3},{8,12},{9,13},{10,... | collective-permute-start | bytes 983048 | tf_op jit(solution)/shard_map/ppermute | solution.py:1235
  21.1 23.4 %collective-permute-start.5 = (bf16[64,2560]{1,0:T(8,128)(2,1)S(1)}, bf16[64,2560]{1,0:T(8,128)(2,1)}, u32[]{:S(2)}, u32[]{:S(2)}) collective-permute-start(bf16[64,2560]{1,0:T(8,128)(2,1)S(1)} %constant_dynamic-update-slice_fusion.refs_0_), channel_id=1, source_target_pairs={{0,6},{1,7},{2,4},{3,5},{4,2},{5,3},{6,0},{7,1},{8,14},{9,15},{10,... | collective-permute-start | bytes 983048 | tf_op jit(solution)/shard_map/ppermute | solution.py:1235
  37.5 14.2 %collective-permute-start.11 = (bf16[64,128]{1,0:T(8,128)(2,1)}, bf16[64,128]{1,0:T(8,128)(2,1)}, u32[]{:S(2)}, u32[]{:S(2)}) collective-permute-start(bf16[64,128]{1,0:T(8,128)(2,1)} %copy.186), channel_id=1, source_target_pairs={{0,1},{1,0},{2,3},{3,2},{4,5},{5,4},{6,7},{7,6},{8,9},{9,8},{10,11... | collective-permute-start | bytes 49160 | tf_op jit(solution)/shard_map/ppermute | solution.py:1235
  37.5 16.6 %collective-permute-start.12 = (bf16[64,128]{1,0:T(8,128)(2,1)}, bf16[64,128]{1,0:T(8,128)(2,1)}, u32[]{:S(2)}, u32[]{:S(2)}) collective-permute-start(bf16[64,128]{1,0:T(8,128)(2,1)} %copy.186), channel_id=1, source_target_pairs={{0,2},{1,3},{2,0},{3,1},{4,6},{5,7},{6,4},{7,5},{8,10},{9,11},{10,... | collective-permute-start | bytes 49160 | tf_op jit(solution)/shard_map/ppermute | solution.py:1235
  38.4 15.8 %collective-permute-start.14 = (bf16[64,128]{1,0:T(8,128)(2,1)}, bf16[64,128]{1,0:T(8,128)(2,1)}, u32[]{:S(2)}, u32[]{:S(2)}) collective-permute-start(bf16[64,128]{1,0:T(8,128)(2,1)} %copy.186), channel_id=1, source_target_pairs={{0,4},{1,5},{2,6},{3,7},{4,0},{5,1},{6,2},{7,3},{8,12},{9,13},{10,... | collective-permute-start | bytes 49160 | tf_op jit(solution)/shard_map/ppermute | solution.py:1235
  47.6 40.8 %collective-permute-start.9 = (bf16[4,64,2560]{2,1,0:T(8,128)(2,1)}, bf16[4,64,2560]{2,1,0:T(8,128)(2,1)}, u32[]{:S(2)}, u32[]{:S(2)}) collective-permute-start(bf16[4,64,2560]{2,1,0:T(8,128)(2,1)} %stack_weights.1.w0), channel_id=1, source_target_pairs={{0,8},{8,0},{16,24},{24,16},{1,9},{9,1},{17,25},{25,17},{2,10},{10... | collective-permute-start | bytes 3932168 | tf_op jit(solution)/shard_map/ppermute | solution.py:1238
  49.0 39.3 %collective-permute-start.10 = (bf16[4,64,2560]{2,1,0:T(8,128)(2,1)}, bf16[4,64,2560]{2,1,0:T(8,128)(2,1)}, u32[]{:S(2)}, u32[]{:S(2)}) collective-permute-start(bf16[4,64,2560]{2,1,0:T(8,128)(2,1)} %stack_weights.1.w0), channel_id=1, source_target_pairs={{0,16},{8,24},{16,0},{24,8},{1,17},{9,25},{17,1},{25,9},{2,18},{10... | collective-permute-start | bytes 3932168 | tf_op jit(solution)/shard_map/ppermute | solution.py:1238
  51.7 5.8 %collective-permute-start.16 = (bf16[64,128]{1,0:T(8,128)(2,1)}, bf16[64,128]{1,0:T(8,128)(2,1)S(1)}, u32[]{:S(2)}, u32[]{:S(2)}) collective-permute-start(bf16[64,128]{1,0:T(8,128)(2,1)} %copy.186), channel_id=1, source_target_pairs={{0,6},{1,7},{2,4},{3,5},{4,2},{5,3},{6,0},{7,1},{8,14},{9,15},{10,... | collective-permute-start | bytes 49160 | tf_op jit(solution)/shard_map/ppermute | solution.py:1235
  54.1 15.5 %collective-permute-start.13 = (bf16[64,128]{1,0:T(8,128)(2,1)}, bf16[64,128]{1,0:T(8,128)(2,1)S(1)}, u32[]{:S(2)}, u32[]{:S(2)}) collective-permute-start(bf16[64,128]{1,0:T(8,128)(2,1)} %collective-permute-done.12.refs_2_), channel_id=1, source_target_pairs={{0,1},{1,0},{2,3},{3,2},{4,5},{5,4},{6,7},{7,6},{8,9},{9,8},{10,11... | collective-permute-start | bytes 49160 | tf_op jit(solution)/shard_map/ppermute | solution.py:1235
  54.2 16.0 %collective-permute-start.15 = (bf16[64,128]{1,0:T(8,128)(2,1)}, bf16[64,128]{1,0:T(8,128)(2,1)S(1)}, u32[]{:S(2)}, u32[]{:S(2)}) collective-permute-start(bf16[64,128]{1,0:T(8,128)(2,1)} %collective-permute-done.14.refs_4_), channel_id=1, source_target_pairs={{0,1},{1,0},{2,3},{3,2},{4,5},{5,4},{6,7},{7,6},{8,9},{9,8},{10,11... | collective-permute-start | bytes 49160 | tf_op jit(solution)/shard_map/ppermute | solution.py:1235
  57.5 13.2 %collective-permute-start.17 = (bf16[64,128]{1,0:T(8,128)(2,1)S(1)}, bf16[64,128]{1,0:T(8,128)(2,1)S(1)}, u32[]{:S(2)}, u32[]{:S(2)}) collective-permute-start(bf16[64,128]{1,0:T(8,128)(2,1)S(1)} %collective-permute-done.16.refs_6_), channel_id=1, source_target_pairs={{0,1},{1,0},{2,3},{3,2},{4,5},{5,4},{6,7},{7,6},{8,9},{9,8},{10,11... | collective-permute-start | bytes 49160 | tf_op jit(solution)/shard_map/ppermute | solution.py:1235
  69.6 14.6 %collective-permute-start.6 = (bf16[1024,128]{1,0:T(8,128)(2,1)}, bf16[1024,128]{1,0:T(8,128)(2,1)S(1)}, u32[]{:S(2)}, u32[]{:S(2)}) collective-permute-start(bf16[1024,128]{1,0:T(8,128)(2,1)} %gather_fusion.1), channel_id=1, source_target_pairs={{0,8},{8,0},{16,24},{24,16},{1,9},{9,1},{17,25},{25,17},{2,10},{10... | collective-permute-start | bytes 786440 | tf_op jit(solution)/shard_map/ppermute | solution.py:1238
  70.3 18.1 %collective-permute-start.7 = (bf16[1024,128]{1,0:T(8,128)(2,1)}, bf16[1024,128]{1,0:T(8,128)(2,1)S(1)}, u32[]{:S(2)}, u32[]{:S(2)}) collective-permute-start(bf16[1024,128]{1,0:T(8,128)(2,1)} %gather_fusion.2), channel_id=1, source_target_pairs={{0,16},{8,24},{16,0},{24,8},{1,17},{9,25},{17,1},{25,9},{2,18},{10... | collective-permute-start | bytes 786440 | tf_op jit(solution)/shard_map/ppermute | solution.py:1238
  70.8 17.6 %collective-permute-start.8 = (bf16[1024,128]{1,0:T(8,128)(2,1)S(1)}, bf16[1024,128]{1,0:T(8,128)(2,1)S(1)}, u32[]{:S(2)}, u32[]{:S(2)}) collective-permute-start(bf16[1024,128]{1,0:T(8,128)(2,1)S(1)} %gather_fusion.3), channel_id=1, source_target_pairs={{0,24},{8,16},{16,8},{24,0},{1,25},{9,17},{17,9},{25,1},{2,26},{10... | collective-permute-start | bytes 786440 | tf_op jit(solution)/shard_map/ppermute | solution.py:1238
  88.4 246.3 %reduce-scatter.7.cloned.1.call-start = ((), (), s32[]{:S(2)}) async-start(), calls=%async_computation.5 | async-start | bytes 8048640
  104.2 6.1 %collective-permute-start.18 = (bf16[2,256,128]{2,1,0:T(8,128)(2,1)S(1)}, bf16[2,256,128]{2,1,0:T(8,128)(2,1)S(1)}, u32[]{:S(2)}, u32[]{:S(2)}) collective-permute-start(bf16[2,256,128]{2,1,0:T(8,128)(2,1)S(1)} %constant_dynamic-slice_fusion.2), channel_id=1, source_target_pairs={{0,1},{1,0},{2,3},{3,2},{4,5},{5,4},{6,7},{7,6},{8,9},{9,8},{10,11... | collective-permute-start | bytes 393224 | tf_op jit(solution)/shard_map/ppermute | solution.py:1235
  106.2 40.0 %collective-permute-start.22 = (bf16[2,64,2560]{2,1,0:T(8,128)(2,1)}, bf16[2,64,2560]{2,1,0:T(8,128)(2,1)S(1)}, u32[]{:S(2)}, u32[]{:S(2)}) collective-permute-start(bf16[2,64,2560]{2,1,0:T(8,128)(2,1)} %slice.179), channel_id=1, source_target_pairs={{0,16},{8,24},{16,0},{24,8},{1,17},{9,25},{17,1},{25,9},{2,18},{10... | collective-permute-start | bytes 1966088 | tf_op jit(solution)/shard_map/ppermute | solution.py:1238
  109.7 36.5 %collective-permute-start.23 = (bf16[2,64,2560]{2,1,0:T(8,128)(2,1)}, bf16[2,64,2560]{2,1,0:T(8,128)(2,1)}, u32[]{:S(2)}, u32[]{:S(2)}) collective-permute-start(bf16[2,64,2560]{2,1,0:T(8,128)(2,1)} %slice.180), channel_id=1, source_target_pairs={{0,8},{8,0},{16,24},{24,16},{1,9},{9,1},{17,25},{25,17},{2,10},{10... | collective-permute-start | bytes 1966088 | tf_op jit(solution)/shard_map/ppermute | solution.py:1238
  111.1 22.2 %collective-permute-start.19 = (bf16[1536,128]{1,0:T(8,128)(2,1)}, bf16[1536,128]{1,0:T(8,128)(2,1)}, u32[]{:S(2)}, u32[]{:S(2)}) collective-permute-start(bf16[1536,128]{1,0:T(8,128)(2,1)} %pad_maximum_fusion.2.refs_0_), channel_id=1, source_target_pairs={{0,2},{1,3},{2,0},{3,1},{4,6},{5,7},{6,4},{7,5},{8,10},{9,11},{10,... | collective-permute-start | bytes 1179656 | tf_op jit(solution)/shard_map/ppermute | solution.py:1235
  116.1 30.1 %collective-permute-start.20 = (bf16[1536,128]{1,0:T(8,128)(2,1)}, bf16[1536,128]{1,0:T(8,128)(2,1)}, u32[]{:S(2)}, u32[]{:S(2)}) collective-permute-start(bf16[1536,128]{1,0:T(8,128)(2,1)} %pad_maximum_fusion.2.refs_0_), channel_id=1, source_target_pairs={{0,4},{1,5},{2,6},{3,7},{4,0},{5,1},{6,2},{7,3},{8,12},{9,13},{10,... | collective-permute-start | bytes 1179656 | tf_op jit(solution)/shard_map/ppermute | solution.py:1235
  117.1 29.1 %collective-permute-start.21 = (bf16[1536,128]{1,0:T(8,128)(2,1)}, bf16[1536,128]{1,0:T(8,128)(2,1)}, u32[]{:S(2)}, u32[]{:S(2)}) collective-permute-start(bf16[1536,128]{1,0:T(8,128)(2,1)} %pad_maximum_fusion.2.refs_0_), channel_id=1, source_target_pairs={{0,6},{1,7},{2,4},{3,5},{4,2},{5,3},{6,0},{7,1},{8,14},{9,15},{10,... | collective-permute-start | bytes 1179656 | tf_op jit(solution)/shard_map/ppermute | solution.py:1235
  146.8 13.6 %collective-permute-start.28 = (bf16[4,64,2560]{2,1,0:T(8,128)(2,1)}, bf16[4,64,2560]{2,1,0:T(8,128)(2,1)}, u32[]{:S(2)}, u32[]{:S(2)}) collective-permute-start(bf16[4,64,2560]{2,1,0:T(8,128)(2,1)} %stack_weights.1.w0), channel_id=1, source_target_pairs={{0,1},{1,0},{2,3},{3,2},{4,5},{5,4},{6,7},{7,6},{8,9},{9,8},{10,11... | collective-permute-start | bytes 3932168 | tf_op jit(solution)/shard_map/ppermute | solution.py:1235
  146.9 13.5 %collective-permute-start.29 = (bf16[4,64,2560]{2,1,0:T(8,128)(2,1)}, bf16[4,64,2560]{2,1,0:T(8,128)(2,1)}, u32[]{:S(2)}, u32[]{:S(2)}) collective-permute-start(bf16[4,64,2560]{2,1,0:T(8,128)(2,1)} %collective-permute-done.9.w1), channel_id=1, source_target_pairs={{0,1},{1,0},{2,3},{3,2},{4,5},{5,4},{6,7},{7,6},{8,9},{9,8},{10,11... | collective-permute-start | bytes 3932168 | tf_op jit(solution)/shard_map/ppermute | solution.py:1235
  147.3 13.1 %collective-permute-start.30 = (bf16[4,64,2560]{2,1,0:T(8,128)(2,1)}, bf16[4,64,2560]{2,1,0:T(8,128)(2,1)}, u32[]{:S(2)}, u32[]{:S(2)}) collective-permute-start(bf16[4,64,2560]{2,1,0:T(8,128)(2,1)} %collective-permute-done.10.w2), channel_id=1, source_target_pairs={{0,1},{1,0},{2,3},{3,2},{4,5},{5,4},{6,7},{7,6},{8,9},{9,8},{10,11... | collective-permute-start | bytes 3932168 | tf_op jit(solution)/shard_map/ppermute | solution.py:1235
  148.2 3.6 collective-permute-start.26
  149.4 3.6 collective-permute-start.27
  151.8 8.6 %collective-permute-start.31 = (bf16[2,64,2560]{2,1,0:T(8,128)(2,1)S(1)}, bf16[2,64,2560]{2,1,0:T(8,128)(2,1)}, u32[]{:S(2)}, u32[]{:S(2)}) collective-permute-start(bf16[2,64,2560]{2,1,0:T(8,128)(2,1)S(1)} %collective-permute-done.22.w3), channel_id=1, source_target_pairs={{0,1},{1,0},{2,3},{3,2},{4,5},{5,4},{6,7},{7,6},{8,9},{9,8},{10,11... | collective-permute-start | bytes 1966088 | tf_op jit(solution)/shard_map/ppermute | solution.py:1235
  153.7 6.7 %collective-permute-start.32 = (bf16[2,64,2560]{2,1,0:T(8,128)(2,1)}, bf16[2,64,2560]{2,1,0:T(8,128)(2,1)}, u32[]{:S(2)}, u32[]{:S(2)}) collective-permute-start(bf16[2,64,2560]{2,1,0:T(8,128)(2,1)} %collective-permute-done.23.w4), channel_id=1, source_target_pairs={{0,1},{1,0},{2,3},{3,2},{4,5},{5,4},{6,7},{7,6},{8,9},{9,8},{10,11... | collective-permute-start | bytes 1966088 | tf_op jit(solution)/shard_map/ppermute | solution.py:1235
  172.8 7.2 %collective-permute-start.33 = (bf16[2,256,128]{2,1,0:T(8,128)(2,1)S(1)}, bf16[2,256,128]{2,1,0:T(8,128)(2,1)S(1)}, u32[]{:S(2)}, u32[]{:S(2)}) collective-permute-start(bf16[2,256,128]{2,1,0:T(8,128)(2,1)S(1)} %convert_element_type.111), channel_id=1, source_target_pairs={{0,1},{1,0},{2,3},{3,2},{4,5},{5,4},{6,7},{7,6},{8,9},{9,8},{10,11... | collective-permute-start | bytes 393224 | tf_op jit(solution)/shard_map/ppermute | solution.py:1235
  193.4 6.9 %collective-permute-start.34 = (bf16[2,256,128]{2,1,0:T(8,128)(2,1)S(1)}, bf16[2,256,128]{2,1,0:T(8,128)(2,1)S(1)}, u32[]{:S(2)}, u32[]{:S(2)}) collective-permute-start(bf16[2,256,128]{2,1,0:T(8,128)(2,1)S(1)} %convert_element_type.112), channel_id=1, source_target_pairs={{0,1},{1,0},{2,3},{3,2},{4,5},{5,4},{6,7},{7,6},{8,9},{9,8},{10,11... | collective-permute-start | bytes 393224 | tf_op jit(solution)/shard_map/ppermute | solution.py:1235
  211.7 11.3 %collective-permute-start.35 = (f32[8,256]{1,0:T(8,128)}, f32[8,256]{1,0:T(8,128)S(1)}, u32[]{:S(2)}, u32[]{:S(2)}) collective-permute-start(f32[8,256]{1,0:T(8,128)} %get-tuple-element.192), channel_id=1, source_target_pairs={{0,1},{1,0},{2,3},{3,2},{4,5},{5,4},{6,7},{7,6},{8,9},{9,8},{10,11... | collective-permute-start | bytes 24584 | tf_op jit(solution)/shard_map/ppermute | solution.py:1235
  212.1 10.8 %collective-permute-start.36 = (f32[8,256]{1,0:T(8,128)}, f32[8,256]{1,0:T(8,128)S(1)}, u32[]{:S(2)}, u32[]{:S(2)}) collective-permute-start(f32[8,256]{1,0:T(8,128)} %get-tuple-element.192), channel_id=1, source_target_pairs={{0,2},{1,3},{2,0},{3,1},{4,6},{5,7},{6,4},{7,5},{8,10},{9,11},{10,... | collective-permute-start | bytes 24584 | tf_op jit(solution)/shard_map/ppermute | solution.py:1235
  220.5 4.8 collective-permute-start.38
  221.5 5.7 %collective-permute-start.40 = (f32[8,256]{1,0:T(8,128)}, f32[8,256]{1,0:T(8,128)S(1)}, u32[]{:S(2)}, u32[]{:S(2)}) collective-permute-start(f32[8,256]{1,0:T(8,128)} %get-tuple-element.192), channel_id=1, source_target_pairs={{0,6},{1,7},{2,4},{3,5},{4,2},{5,3},{6,0},{7,1},{8,14},{9,15},{10,... | collective-permute-start | bytes 24584 | tf_op jit(solution)/shard_map/ppermute | solution.py:1235
  223.0 4.2 collective-permute-start.37
  237.8 238.7 %reduce-scatter.9.cloned.1.call-start = ((), (), s32[]{:S(2)}) async-start(), calls=%async_computation.6 | async-start | bytes 8048640
  240.5 9.4 %collective-permute-start.43 = (bf16[2,256,128]{2,1,0:T(8,128)(2,1)S(1)}, bf16[2,256,128]{2,1,0:T(8,128)(2,1)S(1)}, u32[]{:S(2)}, u32[]{:S(2)}) collective-permute-start(bf16[2,256,128]{2,1,0:T(8,128)(2,1)S(1)} %add_convert_fusion.1), channel_id=1, source_target_pairs={{0,2},{1,3},{2,0},{3,1},{4,6},{5,7},{6,4},{7,5},{8,10},{9,11},{10,... | collective-permute-start | bytes 393224 | tf_op jit(solution)/shard_map/ppermute | solution.py:1235
  240.8 12.9 %collective-permute-start.44 = (bf16[2,256,128]{2,1,0:T(8,128)(2,1)S(1)}, bf16[2,256,128]{2,1,0:T(8,128)(2,1)S(1)}, u32[]{:S(2)}, u32[]{:S(2)}) collective-permute-start(bf16[2,256,128]{2,1,0:T(8,128)(2,1)S(1)} %add_convert_fusion.1), channel_id=1, source_target_pairs={{0,4},{1,5},{2,6},{3,7},{4,0},{5,1},{6,2},{7,3},{8,12},{9,13},{10,... | collective-permute-start | bytes 393224 | tf_op jit(solution)/shard_map/ppermute | solution.py:1235
  242.6 11.1 %collective-permute-start.45 = (bf16[2,256,128]{2,1,0:T(8,128)(2,1)S(1)}, bf16[2,256,128]{2,1,0:T(8,128)(2,1)S(1)}, u32[]{:S(2)}, u32[]{:S(2)}) collective-permute-start(bf16[2,256,128]{2,1,0:T(8,128)(2,1)S(1)} %add_convert_fusion.1), channel_id=1, source_target_pairs={{0,6},{1,7},{2,4},{3,5},{4,2},{5,3},{6,0},{7,1},{8,14},{9,15},{10,... | collective-permute-start | bytes 393224 | tf_op jit(solution)/shard_map/ppermute | solution.py:1235
  318.7 8.3 %collective-permute-start.51 = (f32[280,128]{1,0:T(8,128)S(1)}, f32[280,128]{1,0:T(8,128)S(1)}, u32[]{:S(2)}, u32[]{:S(2)}) collective-permute-start(f32[280,128]{1,0:T(8,128)S(1)} %dynamic-slice_add_fusion), channel_id=1, source_target_pairs={{0,2},{1,3},{2,0},{3,1},{4,6},{5,7},{6,4},{7,5},{8,10},{9,11},{10,... | collective-permute-start | bytes 430088 | tf_op jit(solution)/shard_map/ppermute | solution.py:1235
  321.0 13.7 %collective-permute-start.52 = (f32[280,128]{1,0:T(8,128)S(1)}, f32[280,128]{1,0:T(8,128)S(1)}, u32[]{:S(2)}, u32[]{:S(2)}) collective-permute-start(f32[280,128]{1,0:T(8,128)S(1)} %dynamic-slice_add_fusion), channel_id=1, source_target_pairs={{0,4},{1,5},{2,6},{3,7},{4,0},{5,1},{6,2},{7,3},{8,12},{9,13},{10,... | collective-permute-start | bytes 430088 | tf_op jit(solution)/shard_map/ppermute | solution.py:1235
  321.3 13.4 %collective-permute-start.53 = (f32[280,128]{1,0:T(8,128)S(1)}, f32[280,128]{1,0:T(8,128)S(1)}, u32[]{:S(2)}, u32[]{:S(2)}) collective-permute-start(f32[280,128]{1,0:T(8,128)S(1)} %dynamic-slice_add_fusion), channel_id=1, source_target_pairs={{0,6},{1,7},{2,4},{3,5},{4,2},{5,3},{6,0},{7,1},{8,14},{9,15},{10,... | collective-permute-start | bytes 430088 | tf_op jit(solution)/shard_map/ppermute | solution.py:1235
  449.4 22.2 %all-to-all-start.1 = ((bf16[4,1376,128]{2,1,0:T(8,128)(2,1)}), bf16[4,1376,128]{2,1,0:T(8,128)(2,1)}, u32[]{:S(2)}, u32[]{:S(2)}) async-start(bf16[4,1376,128]{2,1,0:T(8,128)(2,1)} %constant_dynamic-update-slice_fusion.13.refs_2_), calls=%async_computation.1 | async-start | bytes 2818048 | tf_op jit(solution)/shard_map/all_to_all | solution.py:1604
  (68 other events, 546.9 us)
Sparse Core Ops, SparseCore 0:
  88.5 88.2 all-gather.2
  238.0 70.0 reduce-scatter.6
  368.0 82.1 reduce-scatter.8
where the time goes:
time: 497 us; the launch traced here: 491 us
  Pallas kernels  245 us (49%)
  waiting for transfers between devices  63.7 us (13%)
  starting transfers between devices  60.8 us (12%)
  local copies, waits for them, and re-layouts  51.7 us (10%)
  blocking collectives  25.4 us (5%)
  other arithmetic  24.1 us (5%)
  between operations  19.6 us (4%)
    pallas_call x16, Pallas kernels, call(): pl.pallas_call(kernel, out_shape=outs, in_specs=[SM if i < smem else ANY...  146 us
    ppermute x45, waiting for transfers between devices, over_wide(): return lax.ppermute(value, WIDE_AXES, [(i, i ^ k) for i in range(width)])  51.5 us
    ppermute x45, starting transfers between devices, over_wide(): return lax.ppermute(value, WIDE_AXES, [(i, i ^ k) for i in range(width)])  42.6 us
    pallas_call x2, Pallas kernels, embed_pass(): pl.pallas_call(partial(embed_kernel, start, vr), grid=(tiles,), in_specs=...  36.7 us
    pallas_call x1, Pallas kernels, unembed_pass(): pl.pallas_call(unembed_kernel, grid=(count,), in_specs=[SM, pl.BlockSpec(...  27.5 us
    all_to_all x1, blocking collectives, body(): extra = lax.all_to_all(extra, 'rep', 0, 0, tiled=True)  25.4 us
    gather x4, local copies, waits for them, and re-layouts, body(): tables[0].at[slot_ids[k].reshape(-1)].get(mode='promise_in_bounds')  16.1 us
    unnamed x151, local copies, waits for them, and re-layouts  14.4 us
  transfers between devices with their start and end apart: 59, of which 23 were waited for; matrix products, arithmetic and copies ran while one was open for 12% of the time, Pallas kernels for 37%

commit v1 on v0

--- a/solution.py
+++ b/solution.py
@@ -1018,7 +1018,7 @@
     start, last, clip_ref, count_ref, at_ref, id_ref, col_ref, rows_ref, first_ref, second_ref, base_ref,
     *refs,
 ):
-    one_ref, two_ref, extra_ref, scr, extra_scr = refs[-5:]
+    one_ref, two_ref, extra_out, scr, extra_scr, extra_ref = refs[-6:]
     tile = one_ref.shape[2]
     first = (pl.program_id(0) + start) * tile
     place = lax.broadcasted_iota(jnp.int32, (tile, 1), 0) + first
@@ -1048,6 +1048,10 @@
             extra_ref[r, part, :] += picked[:, LANES * r : LANES * (r + 1)]
 
     overlapping(lambda k: at_ref[k], count_ref[0], first, tile, scatter)
+
+    @pl.when(pl.program_id(0) == pl.num_programs(0) - 1)
+    def _():
+        extra_out[...] = extra_ref[...].astype(BF)
 
 
 def embed_pass(clip, count, ids, rows, first, second, base, held, after, start, tiles):
@@ -1072,9 +1076,13 @@
         ]
         + [ANY] * 3,
         out_specs=[whole, whole, blocks],
-        out_shape=[shaped(*first.shape)] * 2 + [shaped(BLOCKS, n_slots, LANES)],
+        out_shape=[shaped(*first.shape)] * 2 + [shaped(BLOCKS, n_slots, LANES, kind=BF)],
         input_output_aliases={9: 0, 10: 1},
-        scratch_shapes=[pltpu.VMEM((TILE, D), F4), pltpu.VMEM((TILE, D), BF)],
+        scratch_shapes=[
+            pltpu.VMEM((TILE, D), F4),
+            pltpu.VMEM((TILE, D), BF),
+            pltpu.VMEM((BLOCKS, n_slots, LANES), F4),
+        ],
         compiler_params=params(),
         name="embedding_adam",
         cost_estimate=takes(17),
@@ -1166,26 +1174,25 @@
     )(counts, ids.reshape(reps, -1), ids, extra, base, master, outer, *held)
 
 
-def unembed_settle_kernel(reps, rate, sum_ref, master_ref, outer_ref, *refs):
-    new_ref, mom_ref = refs[-2:]
-    rows = sum_ref.shape[0]
-    new_ref[0, :rows], mom_ref[0, :rows] = settle(
-        sum_ref[...].astype(F4), master_ref[0, :rows], outer_ref[0, :rows], rate, reps
-    )
-
-
-def unembed_settle(reps, total, master, outer, held, piece, size):
-    whole = pl.BlockSpec((1, size, LANES), lambda i: (1, piece, 0))
+def unembed_settle_kernel(reps, rate, sum_ref, master_ref, outer_ref, held_one, held_two, *refs):
+    new_ref, mom_ref = refs
+    new_ref[0], mom_ref[0] = settle(
+        sum_ref[...].astype(F4), master_ref[0], outer_ref[0], rate, reps
+    )
+
+
+def unembed_settle(reps, total, master, outer, held):
+    whole = pl.BlockSpec((1, SETTLE, LANES), lambda i: (1, i, 0))
     return pl.pallas_call(
         partial(unembed_settle_kernel, reps, LEARN_RATES[0]),
-        grid=(1,),
-        in_specs=[pl.BlockSpec(total.shape, lambda i: (0, 0)), whole, whole] + [ANY] * len(held),
+        grid=(pl.cdiv(total.shape[0], SETTLE),),
+        in_specs=[pl.BlockSpec((SETTLE, LANES), lambda i: (i, 0)), whole, whole, ANY, ANY],
         out_specs=[whole, whole],
         out_shape=[shaped(*master.shape)] * 2,
-        input_output_aliases={3 + i: i for i in range(len(held))},
+        input_output_aliases={3: 0, 4: 1},
         compiler_params=params(),
         name="unembedding_settle",
-        cost_estimate=takes(3),
+        cost_estimate=takes(5),
     )(total, master, outer, *held)
 
 
@@ -1605,15 +1612,13 @@
     packed = jnp.sum(packed.astype(F4), axis=0)
 
     e_tiles = pl.cdiv(vr, TILE)
-    e_pieces = min(2, e_tiles)
+    e_pieces = 1
     e_bounds = [e_tiles * i // e_pieces for i in range(e_pieces + 1)]
-    extra = 0.0
     for i in range(e_pieces):
-        *held, part = embed_pass(
+        *held, extra = embed_pass(
             clip, row_count.reshape(1), row_ids, grad_rows, first_tables, second_tables, base_step, held,
             steps, e_bounds[i], e_bounds[i + 1] - e_bounds[i],
         )
-        extra = extra + part
     one_tables, two_tables = held
     coded = jnp.concatenate([(row_ids + LANES) // LANES, (row_ids + LANES) % LANES])
     coded = jnp.broadcast_to(coded.astype(BF).reshape(1, -1, LANES), (reps, n_slots // 64, LANES))
@@ -1623,18 +1628,11 @@
     coded = coded[:, 0] * LANES + coded[:, 1] - LANES
     counts = jnp.sum((coded >= 0).astype(jnp.int32), axis=1)
 
-    new_tables = ()
-    for i in range(pieces - 1):
-        new_tables = unembed_settle(
-            reps, terms[i], tables, outer_tables, new_tables, i, terms[0].shape[0]
-        )
     new_tables = embed_settle(
         reps, counts, coded.reshape(reps, n_slots // GROUP, 1, GROUP), extra, base_sum, tables,
-        outer_tables, new_tables,
-    )
-    new_tables = unembed_settle(
-        reps, terms[-1], tables, outer_tables, new_tables, pieces - 1, terms[0].shape[0]
-    )
+        outer_tables, (),
+    )
+    new_tables = unembed_settle(reps, terms[0], tables, outer_tables, new_tables)
 
     cols = FF // BLOCKS // LANES
     at_ff = 2 * L * own_rows

time: 497 us -> 492 us (0.990)
  starting transfers between devices: 60.8 us -> 51.5 us
  waiting for transfers between devices: 63.7 us -> 72.5 us
  Pallas kernels: 245 us -> 238 us
    ppermute x45, starting transfers between devices: 42.6 us -> 32.6 us  [over_wide(): return lax.ppermute(value, WIDE_AXES, [(i, i ^ k) for i in range(width)])]
    ppermute x10, waiting for transfers between devices: 10.5 us -> 16.1 us  [over_rep(): return lax.ppermute(value, 'rep', [(i, i ^ k) for i in range(reps)])]
    pallas_call x2 -> x1, Pallas kernels: 36.7 us -> 31.3 us  [embed_pass(): pl.pallas_call(partial(embed_kernel, start, vr), grid=(tiles,), in_specs=...]
    unnamed x151 -> x149, local copies, waits for them, and re-layouts: 14.4 us -> 13.6 us
  transfers between devices with their start and end apart: 59 -> 59, of which waited for: 23 -> 22; matrix products, arithmetic and copies ran while one was open for 12% -> 12% of each run, Pallas kernels for 37% -> 35%
where the time goes in v1:
time: 492 us; the launch traced here: 485 us
  Pallas kernels  238 us (48%)
  waiting for transfers between devices  72.5 us (15%)
  starting transfers between devices  51.5 us (10%)
  local copies, waits for them, and re-layouts  50.4 us (10%)
  blocking collectives  29.7 us (6%)
  other arithmetic  23.1 us (5%)
  between operations  19.3 us (4%)
    pallas_call x16, Pallas kernels, call(): pl.pallas_call(kernel, out_shape=outs, in_specs=[SM if i < smem else ANY...  145 us
    ppermute x45, waiting for transfers between devices, over_wide(): return lax.ppermute(value, WIDE_AXES, [(i, i ^ k) for i in range(width)])  53.7 us
    ppermute x45, starting transfers between devices, over_wide(): return lax.ppermute(value, WIDE_AXES, [(i, i ^ k) for i in range(width)])  32.6 us
    pallas_call x1, Pallas kernels, embed_pass(): pl.pallas_call(partial(embed_kernel, start, vr), grid=(tiles,), in_specs=...  31.3 us
    all_to_all x1, blocking collectives, body(): extra = lax.all_to_all(extra, 'rep', 0, 0, tiled=True)  29.7 us
    pallas_call x1, Pallas kernels, unembed_pass(): pl.pallas_call(unembed_kernel, grid=(count,), in_specs=[SM, pl.BlockSpec(...  27.4 us
    gather x4, local copies, waits for them, and re-layouts, body(): tables[0].at[slot_ids[k].reshape(-1)].get(mode='promise_in_bounds')  16.1 us
    ppermute x10, waiting for transfers between devices, over_rep(): return lax.ppermute(value, 'rep', [(i, i ^ k) for i in range(reps)])  16.1 us
  transfers between devices with their start and end apart: 59, of which 22 were waited for; matrix products, arithmetic and copies ran while one was open for 12% of the time, Pallas kernels for 35%

profile of v1, /device:TPU:0, one launch (start us, length us, event | category | flops | bytes accessed | tf_op | source)
XLA Modules:
  0.0 485.0 jit_solution(8596473315406002435)
XLA Ops:
  11.9 4.0 collective-permute-start.2
  16.5 4.0 collective-permute-start.5
  21.1 5.0 %fusion = (bf16[6288,128]{1,0:T(8,128)(2,1)}, bf16[6288,128]{1,0:T(8,128)(2,1)}) fusion(f32[2,6288,128]{2,1,0:T(8,128)} %master_ref.3), kind=kLoop, calls=%fused_computation.7 | loop fusion | bytes 6438912 | tf_op jit(solution)/shard_map/convert_element_type | solution.py:1283
  27.4 7.6 %slots.1 = (s32[4,8,128]{2,1,0:T(8,128)}, s32[8,128]{1,0:T(8,128)}, s32[8,128]{1,0:T(8,128)}, f32[4,24,256]{2,1,0:T(8,128)}) custom-call(s32[8]{0:T(128)} %stack.63.sc_ref, f32[40,256]{1,0:T(8,128)} %copy-done.27, f32[40,256]{1,0:T(8,128)} %collective-permute-done.x_all, f32[40,256]{1,0:T(8,128)} %copy-done.40, f32[40,256]{1,0:T(8,128)} %copy-done.39), custom_call_target="tpu_custom_call" | custom-call | bytes 21000000 | tf_op jit(solution)/shard_map/slots/pallas_call | solution.py:116
  37.6 3.8 collective-permute-start.16
  42.5 6.2 %collective-permute-done.4.refs_2_ = bf16[64,2560]{1,0:T(8,128)(2,1)S(1)} collective-permute-done((bf16[64,2560]{1,0:T(8,128)(2,1)S(1)}, bf16[64,2560]{1,0:T(8,128)(2,1)S(1)}, u32[]{:S(2)}, u32[]{:S(2)}) %collective-permute-start.4) | collective-permute-done | bytes 327712 | tf_op jit(solution)/shard_map/ppermute | solution.py:1242
  49.4 2.4 stack_weights.1.w0
  57.9 3.2 gather_fusion.3
  61.1 4.3 gather_fusion.2
  65.4 4.3 gather_fusion.1
  70.8 2.4 collective-permute-start.8
  73.5 4.3 gather_fusion
  77.8 13.1 %collective-permute-done.6.r1 = bf16[1024,128]{1,0:T(8,128)(2,1)S(1)} collective-permute-done((bf16[1024,128]{1,0:T(8,128)(2,1)}, bf16[1024,128]{1,0:T(8,128)(2,1)S(1)}, u32[]{:S(2)}, u32[]{:S(2)}) %collective-permute-start.6) | collective-permute-done | bytes 262176 | tf_op jit(solution)/shard_map/ppermute | solution.py:1245
  90.9 3.0 collective-permute-done.8.r3
  98.8 3.7 places.1
  103.7 4.0 keys_values.1
  108.8 2.0 slice.179
  118.2 2.9 collective-permute-start.19
  121.0 13.7 %embedding_base.1.after_ref.base_ref = bf16[4,6288,128]{2,1,0:T(8,128)(2,1)} custom-call(f32[1,2,6288,512]{3,2,1,0:T(8,128)} %first_ref.5, f32[1,2,6288,512]{3,2,1,0:T(8,128)} %second_ref.5, bf16[1024,128]{1,0:T(8,128)(2,1)} %get-tuple-element.164.after_ref), custom_call_target="tpu_custom_call" | custom-call | bytes 42000000 | tf_op jit(solution)/shard_map/embedding_base/pallas_call | solution.py:954
  134.7 16.8 %collective-permute-done.20.refs_4_ = bf16[1536,128]{1,0:T(8,128)(2,1)} collective-permute-done((bf16[1536,128]{1,0:T(8,128)(2,1)}, bf16[1536,128]{1,0:T(8,128)(2,1)}, u32[]{:S(2)}, u32[]{:S(2)}) %collective-permute-start.20) | collective-permute-done | bytes 393248 | tf_op jit(solution)/shard_map/ppermute | solution.py:1242
  154.8 2.3 collective-permute-done.26.refs_5_
  158.9 6.6 %token_order.1 = (bf16[16,256,128]{2,1,0:T(8,128)(2,1)}, f32[4,256,128]{2,1,0:T(8,128)}) custom-call(s32[8]{0:T(128)} %stack.63.sc_ref, bf16[4,6288,128]{2,1,0:T(8,128)(2,1)} %embedding_base.1.after_ref.base_ref, s32[16,1,512]{2,1,0:T(1,128)} %get-tuple-element.169.code_ref, bf16[1536,128]{1,0:T(8,128)(2,1)} %pad_maximum_fusion.2.refs_0_, ...), custom_call_target="tpu_custom_call" | custom-call | bytes 15000000 | tf_op jit(solution)/shard_map/token_order/pallas_call | solution.py:116
  165.6 11.3 %first_attention.1 = (f32[256,512]{1,0:T(8,128)}, f32[2,256,128]{2,1,0:T(8,128)}, f32[2,256,128]{2,1,0:T(8,128)}, f32[4,256,1]{2,1,0:T(8,128)}) custom-call(s32[8]{0:T(128)} %stack.63.sc_ref, f32[4,256,128]{2,1,0:T(8,128)} %get-tuple-element.174.low_ref, f32[1,5632]{1,0:T(1,128)} %slice.177.vec_ref, bf16[4,64,2560]{2,1,0:T(8,128)(2,1)} %stack_weights.1.w0, ...), custom_call_target="tpu_custom_call" | custom-call | bytes 27000000 | tf_op jit(solution)/shard_map/first_attention/pallas_call | solution.py:116
  178.7 6.1 %first_feed.1.partial_ref = f32[256,512]{1,0:T(8,128)} custom-call(s32[8]{0:T(128)} %stack.63.sc_ref, f32[256,512]{1,0:T(8,128)} %get-tuple-element.181.stream_ref, f32[1,5632]{1,0:T(1,128)} %slice.177.vec_ref, bf16[4,64,2560]{2,1,0:T(8,128)(2,1)} %stack_weights.1.w0, bf16[4,64,2560]{2,1,0:T(8,128)(2,1)} %collective-permute-done.9.w1, ...), custom_call_target="tpu_custom_call" | custom-call | bytes 15000000 | tf_op jit(solution)/shard_map/first_feed/pallas_call | solution.py:116
  185.4 11.8 %second_attention.1 = (f32[256,512]{1,0:T(8,128)}, f32[2,256,128]{2,1,0:T(8,128)}, f32[2,256,128]{2,1,0:T(8,128)}, f32[4,256,1]{2,1,0:T(8,128)}) custom-call(s32[8]{0:T(128)} %stack.63.sc_ref, f32[256,512]{1,0:T(8,128)} %first_feed.1.partial_ref, f32[2,256,128]{2,1,0:T(8,128)} %get-tuple-element.184.own_ref, bf16[2,256,128]{2,1,0:T(8,128)(2,1)} %copy-done.6, ...), custom_call_target="tpu_custom_call" | custom-call | bytes 27000000 | tf_op jit(solution)/shard_map/second_attention/pallas_call | solution.py:116
  199.2 6.1 %second_feed.1.partial_ref = f32[256,512]{1,0:T(8,128)} custom-call(s32[8]{0:T(128)} %stack.63.sc_ref, f32[256,512]{1,0:T(8,128)} %get-tuple-element.185.stream_ref.stream1_ref, f32[1,5632]{1,0:T(1,128)} %slice.182.vec_ref.vec1_ref, bf16[4,64,2560]{2,1,0:T(8,128)(2,1)} %stack_weights.1.w0, bf16[4,64,2560]{2,1,0:T(8,128)(2,1)} %collective-permute-done.9.w1, ...), custom_call_target="tpu_custom_call" | custom-call | bytes 15000000 | tf_op jit(solution)/shard_map/second_feed/pallas_call | solution.py:116
  206.0 10.7 %logits.1 = (f32[6288,256]{1,0:T(8,128)}, f32[8,256]{1,0:T(8,128)}, f32[256,512]{1,0:T(8,128)}, bf16[256,512]{1,0:T(8,128)(2,1)}) custom-call(s32[8]{0:T(128)} %stack.63.sc_ref, f32[256,512]{1,0:T(8,128)} %second_feed.1.partial_ref, f32[2,256,128]{2,1,0:T(8,128)} %get-tuple-element.186.own_ref, bf16[2,256,128]{2,1,0:T(8,128)(2,1)} %copy-done.7, ...), custom_call_target="tpu_custom_call" | custom-call | bytes 30000000 | tf_op jit(solution)/shard_map/logits/pallas_call | solution.py:116
  216.8 2.5 collective-permute-start.40
  219.2 2.0 collective-permute-start.36
  226.0 8.8 %loss_gradient.1 = (bf16[6288,256]{1,0:T(8,128)(2,1)}, f32[4,256,128]{2,1,0:T(8,128)}, f32[1,1]{1,0:T(1,128)}) custom-call(s32[8]{0:T(128)} %stack.63.sc_ref, f32[8,8,256]{2,1,0:T(8,128)} %copy-done.33, f32[1,256]{1,0:T(1,128)} %get-tuple-element.190.weight_ref, s32[1,256]{1,0:T(1,128)} %get-tuple-element.187.target_ref, ...), custom_call_target="tpu_custom_call" | custom-call | bytes 27000000 | tf_op jit(solution)/shard_map/loss_gradient/pallas_call | solution.py:116
  240.0 2.0 collective-permute-start.43
  242.0 5.0 %squares.1.before_ref = f32[1,1]{1,0:T(1,128)} custom-call(bf16[6288,256]{1,0:T(8,128)(2,1)} %get-tuple-element.195.probs_ref, bf16[256,512]{1,0:T(8,128)(2,1)} %get-tuple-element.196.picked_ref), custom_call_target="tpu_custom_call" | custom-call | bytes 9000000 | tf_op jit(solution)/shard_map/squares/pallas_call | solution.py:116
  247.0 5.0 %collective-permute-done.44 = bf16[2,256,128]{2,1,0:T(8,128)(2,1)S(1)} collective-permute-done((bf16[2,256,128]{2,1,0:T(8,128)(2,1)S(1)}, bf16[2,256,128]{2,1,0:T(8,128)(2,1)S(1)}, u32[]{:S(2)}, u32[]{:S(2)}) %collective-permute-start.44) | collective-permute-done | bytes 131104 | tf_op jit(solution)/shard_map/ppermute | solution.py:1242
  254.5 16.9 %second_pull.1 = (bf16[2,256,128]{2,1,0:T(8,128)(2,1)}, f32[2,2,1024,128]{3,2,1,0:T(8,128)}, f32[2,64,2048]{2,1,0:T(8,128)}, f32[64,512]{1,0:T(8,128)}, f32[1,56...) custom-call(s32[8]{0:T(128)} %stack.63.sc_ref, ...), custom_call_target="tpu_custom_call" | custom-call | bytes 48000000 | tf_op jit(solution)/shard_map/second_pull/pallas_call | solution.py:116
  273.7 23.2 %first_pull.1 = (bf16[2,256,128]{2,1,0:T(8,128)(2,1)}, f32[1024,128]{1,0:T(8,128)}, f32[1024,128]{1,0:T(8,128)}, f32[2,64,2048]{2,1,0:T(8,128)}, f32[64,512]{1,0...) custom-call(s32[8]{0:T(128)} %stack.63.sc_ref, ...), custom_call_target="tpu_custom_call" | custom-call | bytes 69000000 | tf_op jit(solution)/shard_map/first_pull/pallas_call | solution.py:116
  300.1 12.4 %embedding_pull.1 = (f32[64,512]{1,0:T(8,128)}, f32[1,1536]{1,0:T(1,128)}, bf16[1024,512]{1,0:T(8,128)(2,1)}, s32[1024,1]{1,0:T(8,128)}, f32[512,128]{1,0:T(8,12...) custom-call(s32[8]{0:T(128)} %stack.63.sc_ref, f32[256,512]{1,0:T(8,128)} %get-tuple-element.212.grad_in_ref, ...), custom_call_target="tpu_custom_call" | custom-call | bytes 36000000 | tf_op jit(solution)/shard_map/embedding_pull/pallas_call | solution.py:116
  316.6 2.8 collective-permute-start.53
  321.1 4.1 collective-permute-done.53
  325.2 6.0 %collective-permute-done.52 = f32[280,128]{1,0:T(8,128)S(1)} collective-permute-done((f32[280,128]{1,0:T(8,128)S(1)}, f32[280,128]{1,0:T(8,128)S(1)}, u32[]{:S(2)}, u32[]{:S(2)}) %collective-permute-start.52) | collective-permute-done | bytes 143392 | tf_op jit(solution)/shard_map/ppermute | solution.py:1242
  336.8 27.4 %unembedding_adam.1 = (f32[1,2,6288,512]{3,2,1,0:T(8,128)}, f32[1,2,6288,512]{3,2,1,0:T(8,128)}, bf16[4,6288,128]{2,1,0:T(8,128)(2,1)}) custom-call(f32[1]{0:T(128)} %bitcast.55.clip_ref, bf16[6288,256]{1,0:T(8,128)(2,1)} %get-tuple-element.195.probs_ref, bf16[256,512]{1,0:T(8,128)(2,1)} %get-tuple-element.196.picked_ref, f32[1,2,6288,512]{3,2,1,0:T(8,128)} %first_ref.5, ...), custom_call_target="tpu_custom_call" | custom-call | bytes 48000000 | tf_op jit(solution)/shard_map/unembedding_adam/pallas_call | solution.py:980
  368.7 8.5 %layers_adam.1 = (f32[1,2,2,64,512]{4,3,2,1,0:T(8,128)}, f32[1,2,2,64,512]{4,3,2,1,0:T(8,128)}, f32[1,2,2,64,2048]{4,3,2,1,0:T(8,128)}, f32[1,2,2,64,2048]{4,3,2...) custom-call(f32[1]{0:T(128)} %bitcast.55.clip_ref, ...), custom_call_target="tpu_custom_call" | custom-call | bytes 24000000 | tf_op jit(solution)/shard_map/layers_adam/pallas_call | solution.py:116
  377.3 2.7 constant_dynamic-update-slice_fusion.14
  380.6 31.3 %embedding_adam.1 = (f32[1,2,6288,512]{3,2,1,0:T(8,128)}, f32[1,2,6288,512]{3,2,1,0:T(8,128)}, bf16[4,1024,128]{2,1,0:T(8,128)(2,1)}) custom-call(f32[1]{0:T(128)} %bitcast.55.clip_ref, s32[1]{0:T(128)} %bitcast.57.count_ref, s32[1024]{0:T(1024)} %get-tuple-element.340.at_ref, ...), custom_call_target="tpu_custom_call", output_to_operand_aliasing={{0}: (9, {}), {1}: (10, {})} | custom-call | bytes 51000000 | tf_op jit(solution)/shard_map/embedding_adam/pallas_call | solution.py:1063
  413.5 29.7 %all_to_all.10.extra_ref = bf16[4,1040,128]{2,1,0:T(8,128)(2,1)S(1)} all-to-all(bf16[4,1040,128]{2,1,0:T(8,128)(2,1)S(1)} %pad_maximum_fusion), channel_id=1, replica_groups=mesh['rep'=4,'chip'=4,'core'=2] {'rep'}, dimensions={0} | all-to-all | bytes 2129920 | tf_op jit(solution)/shard_map/all_to_all | solution.py:1626
  443.2 4.5 all-to-all-start.1
  449.6 13.4 %embedding_settle.1 = (f32[2,6288,128]{2,1,0:T(8,128)}, f32[2,6288,128]{2,1,0:T(8,128)}) custom-call(s32[4]{0:T(128)} %get-tuple-element.336.count_ref, s32[4,1024]{1,0:T(4,128)} %bitcast.163, s32[4,8,1,128]{3,2,1,0:T(1,128)} %sub.56.id_ref, bf16[4,1040,128]{2,1,0:T(8,128)(2,1)} %copy-done.2, bf16[6288,128]{1,0:T(8,128)(2,1)} %bitcast.154, ...), custom_call_target="tpu_custom_call" | custom-call | bytes 39000000 | tf_op jit(solution)/shard_map/embedding_settle/pallas_call | solution.py:1154
  463.1 2.6 all-to-all-done.1
  470.7 7.5 %unembedding_settle.1 = (f32[2,6288,128]{2,1,0:T(8,128)}, f32[2,6288,128]{2,1,0:T(8,128)}) custom-call(bf16[6288,128]{1,0:T(8,128)(2,1)} %bitcast.155, f32[2,6288,128]{2,1,0:T(8,128)} %master_ref.3, f32[2,6288,128]{2,1,0:T(8,128)} %outer_ref.3, f32[2,6288,128]{2,1,0:T(8,128)} %get-tuple-element.250.held_one, ...), custom_call_target="tpu_custom_call", output_to_operand_aliasing={{0}: (3, {}), {1}: (4, {})} | custom-call | bytes 15000000 | tf_op jit(solution)/shard_map/unembedding_settle/pallas_call | solution.py:1186
  (370 shorter events, 81.9 us)
Async XLA Ops:
  7.2 177.6 %all-gather.3.cloned.1.call-start = ((), (), s32[]{:S(2)}) async-start(), calls=%async_computation.4 | async-start | bytes 8048640 | tf_op jit(solution)/shard_map/all_gather | solution.py:1371
  11.9 8.6 %collective-permute-start.2 = (f32[40,256]{1,0:T(8,128)S(1)}, f32[40,256]{1,0:T(8,128)S(1)}, u32[]{:S(2)}, u32[]{:S(2)}) collective-permute-start(f32[40,256]{1,0:T(8,128)S(1)} %pad_maximum_fusion.5.own_all), channel_id=1, source_target_pairs={{0,24},{8,16},{16,8},{24,0},{1,25},{9,17},{17,9},{25,1},{2,26},{10... | collective-permute-start | bytes 122888 | tf_op jit(solution)/shard_map/ppermute | solution.py:1245
  15.8 10.9 %collective-permute-start.1 = (f32[40,256]{1,0:T(8,128)S(1)}, f32[40,256]{1,0:T(8,128)S(1)}, u32[]{:S(2)}, u32[]{:S(2)}) collective-permute-start(f32[40,256]{1,0:T(8,128)S(1)} %pad_maximum_fusion.5.own_all), channel_id=1, source_target_pairs={{0,16},{8,24},{16,0},{24,8},{1,17},{9,25},{17,1},{25,9},{2,18},{10... | collective-permute-start | bytes 122888 | tf_op jit(solution)/shard_map/ppermute | solution.py:1245
  16.3 11.1 %collective-permute-start = (f32[40,256]{1,0:T(8,128)S(1)}, f32[40,256]{1,0:T(8,128)}, u32[]{:S(2)}, u32[]{:S(2)}) collective-permute-start(f32[40,256]{1,0:T(8,128)S(1)} %pad_maximum_fusion.5.own_all), channel_id=1, source_target_pairs={{0,8},{8,0},{16,24},{24,16},{1,9},{9,1},{17,25},{25,17},{2,10},{10... | collective-permute-start | bytes 122888 | tf_op jit(solution)/shard_map/ppermute | solution.py:1245
  16.5 24.9 %collective-permute-start.5 = (bf16[64,2560]{1,0:T(8,128)(2,1)S(1)}, bf16[64,2560]{1,0:T(8,128)(2,1)S(1)}, u32[]{:S(2)}, u32[]{:S(2)}) collective-permute-start(bf16[64,2560]{1,0:T(8,128)(2,1)S(1)} %constant_dynamic-update-slice_fusion.refs_0_), channel_id=1, source_target_pairs={{0,6},{1,7},{2,4},{3,5},{4,2},{5,3},{6,0},{7,1},{8,14},{9,15},{10,... | collective-permute-start | bytes 983048 | tf_op jit(solution)/shard_map/ppermute | solution.py:1242
  20.5 28.2 %collective-permute-start.4 = (bf16[64,2560]{1,0:T(8,128)(2,1)S(1)}, bf16[64,2560]{1,0:T(8,128)(2,1)S(1)}, u32[]{:S(2)}, u32[]{:S(2)}) collective-permute-start(bf16[64,2560]{1,0:T(8,128)(2,1)S(1)} %constant_dynamic-update-slice_fusion.refs_0_), channel_id=1, source_target_pairs={{0,4},{1,5},{2,6},{3,7},{4,0},{5,1},{6,2},{7,3},{8,12},{9,13},{10,... | collective-permute-start | bytes 983048 | tf_op jit(solution)/shard_map/ppermute | solution.py:1242
  20.5 28.2 %collective-permute-start.3 = (bf16[64,2560]{1,0:T(8,128)(2,1)S(1)}, bf16[64,2560]{1,0:T(8,128)(2,1)}, u32[]{:S(2)}, u32[]{:S(2)}) collective-permute-start(bf16[64,2560]{1,0:T(8,128)(2,1)S(1)} %constant_dynamic-update-slice_fusion.refs_0_), channel_id=1, source_target_pairs={{0,2},{1,3},{2,0},{3,1},{4,6},{5,7},{6,4},{7,5},{8,10},{9,11},{10,... | collective-permute-start | bytes 983048 | tf_op jit(solution)/shard_map/ppermute | solution.py:1242
  37.6 18.4 %collective-permute-start.16 = (bf16[64,128]{1,0:T(8,128)(2,1)}, bf16[64,128]{1,0:T(8,128)(2,1)}, u32[]{:S(2)}, u32[]{:S(2)}) collective-permute-start(bf16[64,128]{1,0:T(8,128)(2,1)} %copy.180), channel_id=1, source_target_pairs={{0,6},{1,7},{2,4},{3,5},{4,2},{5,3},{6,0},{7,1},{8,14},{9,15},{10,... | collective-permute-start | bytes 49160 | tf_op jit(solution)/shard_map/ppermute | solution.py:1242
  41.4 14.9 %collective-permute-start.14 = (bf16[64,128]{1,0:T(8,128)(2,1)}, bf16[64,128]{1,0:T(8,128)(2,1)}, u32[]{:S(2)}, u32[]{:S(2)}) collective-permute-start(bf16[64,128]{1,0:T(8,128)(2,1)} %copy.180), channel_id=1, source_target_pairs={{0,4},{1,5},{2,6},{3,7},{4,0},{5,1},{6,2},{7,3},{8,12},{9,13},{10,... | collective-permute-start | bytes 49160 | tf_op jit(solution)/shard_map/ppermute | solution.py:1242
  41.4 15.5 %collective-permute-start.12 = (bf16[64,128]{1,0:T(8,128)(2,1)}, bf16[64,128]{1,0:T(8,128)(2,1)}, u32[]{:S(2)}, u32[]{:S(2)}) collective-permute-start(bf16[64,128]{1,0:T(8,128)(2,1)} %copy.180), channel_id=1, source_target_pairs={{0,2},{1,3},{2,0},{3,1},{4,6},{5,7},{6,4},{7,5},{8,10},{9,11},{10,... | collective-permute-start | bytes 49160 | tf_op jit(solution)/shard_map/ppermute | solution.py:1242
  51.8 42.1 %collective-permute-start.10 = (bf16[4,64,2560]{2,1,0:T(8,128)(2,1)}, bf16[4,64,2560]{2,1,0:T(8,128)(2,1)}, u32[]{:S(2)}, u32[]{:S(2)}) collective-permute-start(bf16[4,64,2560]{2,1,0:T(8,128)(2,1)} %stack_weights.1.w0), channel_id=1, source_target_pairs={{0,16},{8,24},{16,0},{24,8},{1,17},{9,25},{17,1},{25,9},{2,18},{10... | collective-permute-start | bytes 3932168 | tf_op jit(solution)/shard_map/ppermute | solution.py:1245
  53.3 40.5 %collective-permute-start.9 = (bf16[4,64,2560]{2,1,0:T(8,128)(2,1)}, bf16[4,64,2560]{2,1,0:T(8,128)(2,1)}, u32[]{:S(2)}, u32[]{:S(2)}) collective-permute-start(bf16[4,64,2560]{2,1,0:T(8,128)(2,1)} %stack_weights.1.w0), channel_id=1, source_target_pairs={{0,8},{8,0},{16,24},{24,16},{1,9},{9,1},{17,25},{25,17},{2,10},{10... | collective-permute-start | bytes 3932168 | tf_op jit(solution)/shard_map/ppermute | solution.py:1245
  56.3 13.4 %collective-permute-start.17 = (bf16[64,128]{1,0:T(8,128)(2,1)}, bf16[64,128]{1,0:T(8,128)(2,1)S(1)}, u32[]{:S(2)}, u32[]{:S(2)}) collective-permute-start(bf16[64,128]{1,0:T(8,128)(2,1)} %collective-permute-done.16.refs_6_), channel_id=1, source_target_pairs={{0,1},{1,0},{2,3},{3,2},{4,5},{5,4},{6,7},{7,6},{8,9},{9,8},{10,11... | collective-permute-start | bytes 49160 | tf_op jit(solution)/shard_map/ppermute | solution.py:1242
  56.9 13.4 %collective-permute-start.15 = (bf16[64,128]{1,0:T(8,128)(2,1)}, bf16[64,128]{1,0:T(8,128)(2,1)S(1)}, u32[]{:S(2)}, u32[]{:S(2)}) collective-permute-start(bf16[64,128]{1,0:T(8,128)(2,1)} %collective-permute-done.14.refs_4_), channel_id=1, source_target_pairs={{0,1},{1,0},{2,3},{3,2},{4,5},{5,4},{6,7},{7,6},{8,9},{9,8},{10,11... | collective-permute-start | bytes 49160 | tf_op jit(solution)/shard_map/ppermute | solution.py:1242
  57.5 13.3 %collective-permute-start.13 = (bf16[64,128]{1,0:T(8,128)(2,1)}, bf16[64,128]{1,0:T(8,128)(2,1)S(1)}, u32[]{:S(2)}, u32[]{:S(2)}) collective-permute-start(bf16[64,128]{1,0:T(8,128)(2,1)} %collective-permute-done.12.refs_2_), channel_id=1, source_target_pairs={{0,1},{1,0},{2,3},{3,2},{4,5},{5,4},{6,7},{7,6},{8,9},{9,8},{10,11... | collective-permute-start | bytes 49160 | tf_op jit(solution)/shard_map/ppermute | solution.py:1242
  69.7 21.2 %collective-permute-start.6 = (bf16[1024,128]{1,0:T(8,128)(2,1)}, bf16[1024,128]{1,0:T(8,128)(2,1)S(1)}, u32[]{:S(2)}, u32[]{:S(2)}) collective-permute-start(bf16[1024,128]{1,0:T(8,128)(2,1)} %gather_fusion.1), channel_id=1, source_target_pairs={{0,8},{8,0},{16,24},{24,16},{1,9},{9,1},{17,25},{25,17},{2,10},{10... | collective-permute-start | bytes 786440 | tf_op jit(solution)/shard_map/ppermute | solution.py:1245
  70.3 20.6 %collective-permute-start.7 = (bf16[1024,128]{1,0:T(8,128)(2,1)}, bf16[1024,128]{1,0:T(8,128)(2,1)S(1)}, u32[]{:S(2)}, u32[]{:S(2)}) collective-permute-start(bf16[1024,128]{1,0:T(8,128)(2,1)} %gather_fusion.2), channel_id=1, source_target_pairs={{0,16},{8,24},{16,0},{24,8},{1,17},{9,25},{17,1},{25,9},{2,18},{10... | collective-permute-start | bytes 786440 | tf_op jit(solution)/shard_map/ppermute | solution.py:1245
  70.8 23.1 %collective-permute-start.8 = (bf16[1024,128]{1,0:T(8,128)(2,1)S(1)}, bf16[1024,128]{1,0:T(8,128)(2,1)S(1)}, u32[]{:S(2)}, u32[]{:S(2)}) collective-permute-start(bf16[1024,128]{1,0:T(8,128)(2,1)S(1)} %gather_fusion.3), channel_id=1, source_target_pairs={{0,24},{8,16},{16,8},{24,0},{1,25},{9,17},{17,9},{25,1},{2,26},{10... | collective-permute-start | bytes 786440 | tf_op jit(solution)/shard_map/ppermute | solution.py:1245
  93.9 237.3 %reduce-scatter.7.cloned.1.call-start = ((), (), s32[]{:S(2)}) async-start(), calls=%async_computation.5 | async-start | bytes 8048640
  108.7 7.1 %collective-permute-start.18 = (bf16[2,256,128]{2,1,0:T(8,128)(2,1)S(1)}, bf16[2,256,128]{2,1,0:T(8,128)(2,1)S(1)}, u32[]{:S(2)}, u32[]{:S(2)}) collective-permute-start(bf16[2,256,128]{2,1,0:T(8,128)(2,1)S(1)} %constant_dynamic-slice_fusion.2), channel_id=1, source_target_pairs={{0,1},{1,0},{2,3},{3,2},{4,5},{5,4},{6,7},{7,6},{8,9},{9,8},{10,11... | collective-permute-start | bytes 393224 | tf_op jit(solution)/shard_map/ppermute | solution.py:1242
  112.8 38.7 %collective-permute-start.23 = (bf16[2,64,2560]{2,1,0:T(8,128)(2,1)}, bf16[2,64,2560]{2,1,0:T(8,128)(2,1)S(1)}, u32[]{:S(2)}, u32[]{:S(2)}) collective-permute-start(bf16[2,64,2560]{2,1,0:T(8,128)(2,1)} %slice.180), channel_id=1, source_target_pairs={{0,8},{8,0},{16,24},{24,16},{1,9},{9,1},{17,25},{25,17},{2,10},{10... | collective-permute-start | bytes 1966088 | tf_op jit(solution)/shard_map/ppermute | solution.py:1245
  114.3 37.2 %collective-permute-start.22 = (bf16[2,64,2560]{2,1,0:T(8,128)(2,1)}, bf16[2,64,2560]{2,1,0:T(8,128)(2,1)}, u32[]{:S(2)}, u32[]{:S(2)}) collective-permute-start(bf16[2,64,2560]{2,1,0:T(8,128)(2,1)} %slice.179), channel_id=1, source_target_pairs={{0,16},{8,24},{16,0},{24,8},{1,17},{9,25},{17,1},{25,9},{2,18},{10... | collective-permute-start | bytes 1966088 | tf_op jit(solution)/shard_map/ppermute | solution.py:1245
  116.6 18.1 %collective-permute-start.21 = (bf16[1536,128]{1,0:T(8,128)(2,1)}, bf16[1536,128]{1,0:T(8,128)(2,1)}, u32[]{:S(2)}, u32[]{:S(2)}) collective-permute-start(bf16[1536,128]{1,0:T(8,128)(2,1)} %pad_maximum_fusion.2.refs_0_), channel_id=1, source_target_pairs={{0,6},{1,7},{2,4},{3,5},{4,2},{5,3},{6,0},{7,1},{8,14},{9,15},{10,... | collective-permute-start | bytes 1179656 | tf_op jit(solution)/shard_map/ppermute | solution.py:1242
  118.2 33.3 %collective-permute-start.20 = (bf16[1536,128]{1,0:T(8,128)(2,1)}, bf16[1536,128]{1,0:T(8,128)(2,1)}, u32[]{:S(2)}, u32[]{:S(2)}) collective-permute-start(bf16[1536,128]{1,0:T(8,128)(2,1)} %pad_maximum_fusion.2.refs_0_), channel_id=1, source_target_pairs={{0,4},{1,5},{2,6},{3,7},{4,0},{5,1},{6,2},{7,3},{8,12},{9,13},{10,... | collective-permute-start | bytes 1179656 | tf_op jit(solution)/shard_map/ppermute | solution.py:1242
  118.2 33.3 %collective-permute-start.19 = (bf16[1536,128]{1,0:T(8,128)(2,1)}, bf16[1536,128]{1,0:T(8,128)(2,1)}, u32[]{:S(2)}, u32[]{:S(2)}) collective-permute-start(bf16[1536,128]{1,0:T(8,128)(2,1)} %pad_maximum_fusion.2.refs_0_), channel_id=1, source_target_pairs={{0,2},{1,3},{2,0},{3,1},{4,6},{5,7},{6,4},{7,5},{8,10},{9,11},{10,... | collective-permute-start | bytes 1179656 | tf_op jit(solution)/shard_map/ppermute | solution.py:1242
  151.6 3.0 collective-permute-start.25
  152.1 13.4 %collective-permute-start.28 = (bf16[4,64,2560]{2,1,0:T(8,128)(2,1)}, bf16[4,64,2560]{2,1,0:T(8,128)(2,1)}, u32[]{:S(2)}, u32[]{:S(2)}) collective-permute-start(bf16[4,64,2560]{2,1,0:T(8,128)(2,1)} %stack_weights.1.w0), channel_id=1, source_target_pairs={{0,1},{1,0},{2,3},{3,2},{4,5},{5,4},{6,7},{7,6},{8,9},{9,8},{10,11... | collective-permute-start | bytes 3932168 | tf_op jit(solution)/shard_map/ppermute | solution.py:1242
  152.2 13.4 %collective-permute-start.29 = (bf16[4,64,2560]{2,1,0:T(8,128)(2,1)}, bf16[4,64,2560]{2,1,0:T(8,128)(2,1)}, u32[]{:S(2)}, u32[]{:S(2)}) collective-permute-start(bf16[4,64,2560]{2,1,0:T(8,128)(2,1)} %collective-permute-done.9.w1), channel_id=1, source_target_pairs={{0,1},{1,0},{2,3},{3,2},{4,5},{5,4},{6,7},{7,6},{8,9},{9,8},{10,11... | collective-permute-start | bytes 3932168 | tf_op jit(solution)/shard_map/ppermute | solution.py:1242
  152.6 13.0 %collective-permute-start.30 = (bf16[4,64,2560]{2,1,0:T(8,128)(2,1)}, bf16[4,64,2560]{2,1,0:T(8,128)(2,1)}, u32[]{:S(2)}, u32[]{:S(2)}) collective-permute-start(bf16[4,64,2560]{2,1,0:T(8,128)(2,1)} %collective-permute-done.10.w2), channel_id=1, source_target_pairs={{0,1},{1,0},{2,3},{3,2},{4,5},{5,4},{6,7},{7,6},{8,9},{9,8},{10,11... | collective-permute-start | bytes 3932168 | tf_op jit(solution)/shard_map/ppermute | solution.py:1242
  153.5 3.6 collective-permute-start.26
  154.6 3.6 collective-permute-start.27
  157.1 8.5 %collective-permute-start.31 = (bf16[2,64,2560]{2,1,0:T(8,128)(2,1)}, bf16[2,64,2560]{2,1,0:T(8,128)(2,1)}, u32[]{:S(2)}, u32[]{:S(2)}) collective-permute-start(bf16[2,64,2560]{2,1,0:T(8,128)(2,1)} %collective-permute-done.22.w3), channel_id=1, source_target_pairs={{0,1},{1,0},{2,3},{3,2},{4,5},{5,4},{6,7},{7,6},{8,9},{9,8},{10,11... | collective-permute-start | bytes 1966088 | tf_op jit(solution)/shard_map/ppermute | solution.py:1242
  158.2 7.3 %collective-permute-start.32 = (bf16[2,64,2560]{2,1,0:T(8,128)(2,1)S(1)}, bf16[2,64,2560]{2,1,0:T(8,128)(2,1)}, u32[]{:S(2)}, u32[]{:S(2)}) collective-permute-start(bf16[2,64,2560]{2,1,0:T(8,128)(2,1)S(1)} %collective-permute-done.23.w4), channel_id=1, source_target_pairs={{0,1},{1,0},{2,3},{3,2},{4,5},{5,4},{6,7},{7,6},{8,9},{9,8},{10,11... | collective-permute-start | bytes 1966088 | tf_op jit(solution)/shard_map/ppermute | solution.py:1242
  177.8 7.0 %collective-permute-start.33 = (bf16[2,256,128]{2,1,0:T(8,128)(2,1)S(1)}, bf16[2,256,128]{2,1,0:T(8,128)(2,1)S(1)}, u32[]{:S(2)}, u32[]{:S(2)}) collective-permute-start(bf16[2,256,128]{2,1,0:T(8,128)(2,1)S(1)} %convert_element_type.108), channel_id=1, source_target_pairs={{0,1},{1,0},{2,3},{3,2},{4,5},{5,4},{6,7},{7,6},{8,9},{9,8},{10,11... | collective-permute-start | bytes 393224 | tf_op jit(solution)/shard_map/ppermute | solution.py:1242
  198.2 7.1 %collective-permute-start.34 = (bf16[2,256,128]{2,1,0:T(8,128)(2,1)S(1)}, bf16[2,256,128]{2,1,0:T(8,128)(2,1)S(1)}, u32[]{:S(2)}, u32[]{:S(2)}) collective-permute-start(bf16[2,256,128]{2,1,0:T(8,128)(2,1)S(1)} %convert_element_type.109), channel_id=1, source_target_pairs={{0,1},{1,0},{2,3},{3,2},{4,5},{5,4},{6,7},{7,6},{8,9},{9,8},{10,11... | collective-permute-start | bytes 393224 | tf_op jit(solution)/shard_map/ppermute | solution.py:1242
  216.8 5.7 %collective-permute-start.40 = (f32[8,256]{1,0:T(8,128)}, f32[8,256]{1,0:T(8,128)S(1)}, u32[]{:S(2)}, u32[]{:S(2)}) collective-permute-start(f32[8,256]{1,0:T(8,128)} %get-tuple-element.189), channel_id=1, source_target_pairs={{0,6},{1,7},{2,4},{3,5},{4,2},{5,3},{6,0},{7,1},{8,14},{9,15},{10,... | collective-permute-start | bytes 24584 | tf_op jit(solution)/shard_map/ppermute | solution.py:1242
  219.2 4.8 collective-permute-start.38
  219.2 4.8 collective-permute-start.36
  221.2 3.3 collective-permute-start.35
  222.5 2.9 collective-permute-start.41
  234.9 235.8 %reduce-scatter.9.cloned.1.call-start = ((), (), s32[]{:S(2)}) async-start(), calls=%async_computation.6 | async-start | bytes 8048640
  237.6 9.4 %collective-permute-start.45 = (bf16[2,256,128]{2,1,0:T(8,128)(2,1)S(1)}, bf16[2,256,128]{2,1,0:T(8,128)(2,1)S(1)}, u32[]{:S(2)}, u32[]{:S(2)}) collective-permute-start(bf16[2,256,128]{2,1,0:T(8,128)(2,1)S(1)} %add_convert_fusion), channel_id=1, source_target_pairs={{0,6},{1,7},{2,4},{3,5},{4,2},{5,3},{6,0},{7,1},{8,14},{9,15},{10,... | collective-permute-start | bytes 393224 | tf_op jit(solution)/shard_map/ppermute | solution.py:1242
  239.0 12.9 %collective-permute-start.44 = (bf16[2,256,128]{2,1,0:T(8,128)(2,1)S(1)}, bf16[2,256,128]{2,1,0:T(8,128)(2,1)S(1)}, u32[]{:S(2)}, u32[]{:S(2)}) collective-permute-start(bf16[2,256,128]{2,1,0:T(8,128)(2,1)S(1)} %add_convert_fusion), channel_id=1, source_target_pairs={{0,4},{1,5},{2,6},{3,7},{4,0},{5,1},{6,2},{7,3},{8,12},{9,13},{10,... | collective-permute-start | bytes 393224 | tf_op jit(solution)/shard_map/ppermute | solution.py:1242
  240.0 12.0 %collective-permute-start.43 = (bf16[2,256,128]{2,1,0:T(8,128)(2,1)S(1)}, bf16[2,256,128]{2,1,0:T(8,128)(2,1)S(1)}, u32[]{:S(2)}, u32[]{:S(2)}) collective-permute-start(bf16[2,256,128]{2,1,0:T(8,128)(2,1)S(1)} %add_convert_fusion), channel_id=1, source_target_pairs={{0,2},{1,3},{2,0},{3,1},{4,6},{5,7},{6,4},{7,5},{8,10},{9,11},{10,... | collective-permute-start | bytes 393224 | tf_op jit(solution)/shard_map/ppermute | solution.py:1242
  316.6 8.6 %collective-permute-start.53 = (f32[280,128]{1,0:T(8,128)S(1)}, f32[280,128]{1,0:T(8,128)S(1)}, u32[]{:S(2)}, u32[]{:S(2)}) collective-permute-start(f32[280,128]{1,0:T(8,128)S(1)} %dynamic-slice_add_fusion), channel_id=1, source_target_pairs={{0,6},{1,7},{2,4},{3,5},{4,2},{5,3},{6,0},{7,1},{8,14},{9,15},{10,... | collective-permute-start | bytes 430088 | tf_op jit(solution)/shard_map/ppermute | solution.py:1242
  319.5 11.7 %collective-permute-start.52 = (f32[280,128]{1,0:T(8,128)S(1)}, f32[280,128]{1,0:T(8,128)S(1)}, u32[]{:S(2)}, u32[]{:S(2)}) collective-permute-start(f32[280,128]{1,0:T(8,128)S(1)} %dynamic-slice_add_fusion), channel_id=1, source_target_pairs={{0,4},{1,5},{2,6},{3,7},{4,0},{5,1},{6,2},{7,3},{8,12},{9,13},{10,... | collective-permute-start | bytes 430088 | tf_op jit(solution)/shard_map/ppermute | solution.py:1242
  319.5 11.7 %collective-permute-start.51 = (f32[280,128]{1,0:T(8,128)S(1)}, f32[280,128]{1,0:T(8,128)S(1)}, u32[]{:S(2)}, u32[]{:S(2)}) collective-permute-start(f32[280,128]{1,0:T(8,128)S(1)} %dynamic-slice_add_fusion), channel_id=1, source_target_pairs={{0,2},{1,3},{2,0},{3,1},{4,6},{5,7},{6,4},{7,5},{8,10},{9,11},{10,... | collective-permute-start | bytes 430088 | tf_op jit(solution)/shard_map/ppermute | solution.py:1242
  443.2 22.5 %all-to-all-start.1 = ((bf16[4,1376,128]{2,1,0:T(8,128)(2,1)}), bf16[4,1376,128]{2,1,0:T(8,128)(2,1)}, u32[]{:S(2)}, u32[]{:S(2)}) async-start(bf16[4,1376,128]{2,1,0:T(8,128)(2,1)} %constant_dynamic-update-slice_fusion.13.refs_2_), calls=%async_computation.1 | async-start | bytes 2818048 | tf_op jit(solution)/shard_map/all_to_all | solution.py:1611
  (67 other events, 526.3 us)
Sparse Core Ops, SparseCore 0:
  94.0 77.9 all-gather.2
  235.0 69.7 reduce-scatter.6
  364.4 81.3 reduce-scatter.8
